TPU v7x, 256 devices: a whole 4x4x8 slice. The times are simulated.
256 devices in a mesh: grp: 32 (over z_lo, x, core), tp: 8 (over y, z_hi).
Axes of the slice: x: 4, y: 4, z: 8 (z_hi: 2, z_lo: 4; z = z_hi * 4 + z_lo), core: 2. Of those that a mesh axis runs over, the one named last changes fastest.
Arguments:
- q_attn: bfloat16 [64, 64, 4096], P('grp', None, 'tp'), may hold values from -6 to 6
- q_resid: bfloat16 [64, 64, 4096], P('grp', None, 'tp'), may hold values from -6 to 6
- p_attn: bfloat16 [64, 128, 4096], P('grp', None, 'tp'), may hold values from -6 to 6
- p_resid: bfloat16 [64, 128, 4096], P('grp', None, 'tp'), may hold values from -6 to 6
- w_out: bfloat16 [4096, 4096], P('grp', 'tp'), may hold values from -0.09375 to 0.09375
- w_snap: bfloat16 [4096, 4096], P('grp', 'tp'), may hold values from -0.09375 to 0.09375
- norm_gain: bfloat16 [4096], P('tp'), may hold values from 0.25 to 4
- pass_attn: bfloat16 [64, 256, 4096], P('grp', None, 'tp'), may hold values from -6 to 6
- pass_resid: bfloat16 [64, 256, 4096], P('grp', None, 'tp'), may hold values from -6 to 6
- pass_len: int32 [64], P('grp'), may hold values from 128 to 256, as said below
- block_owner: int32 [32], replicated, may hold values from 0 to 31, each once
- neg_ids: int32 [64, 8], P('grp'), may hold values from 0 to 63
Outputs:
- loss: float32 [], replicated
- w_grad: float32 [4096, 4096], P('grp', 'tp')
- passage_index: bfloat16 [64, 4096], P('grp', 'tp')
Inputs may be any that keep to these rules, and one draw needn't show every extreme that they name: `pass_len`: lengths are multiples of 128; in every block of 2 slots one passage has 256 tokens.
All inputs are finite; a program needn't handle non-finite values.
Results may differ from a plain program's by a relative error of at most 0.0034.
Values may be sent and summed in bfloat16 or wider, within the bound.
A program may use at most 64 MiB of HBM per device.

v0:
```python
import jax
import jax.numpy as jnp
from jax import lax
from jax.sharding import PartitionSpec as P

EPS = 1e-06
TEMP = 0.05


def add_block(tokens, piece):
    return jnp.dot(tokens, piece, preferred_element_type=jnp.float32)


def token_norm(hidden, squares, width, gain):
    factor = lax.rsqrt(squares[:, None] / width + EPS)
    return (factor, hidden * factor * gain[None, :])


def contract_rows(left, right):
    return lax.dot_general(
        left, right, (((0,), (0,)), ((), ())), preferred_element_type=jnp.float32
    )


def spread_tokens(values, count):
    seqs, cols = values.shape
    return jnp.broadcast_to(values[:, None, :], (seqs, count, cols)).reshape(seqs * count, cols)


def shards(
    q_attn,
    q_resid,
    p_attn,
    p_resid,
    w_out,
    w_snap,
    norm_gain,
    pass_attn,
    pass_resid,
    pass_len,
    block_owner,
    neg_ids,
):
    precise = lax.Precision.HIGHEST
    grp_size = lax.axis_size("grp")
    queries, qlen, cols = q_attn.shape
    width = cols * lax.axis_size("tp")
    poslen = p_attn.shape[1]
    blocks, plen = (pass_attn.shape[0], pass_attn.shape[1])
    gain = norm_gain.astype(jnp.float32)
    pass_full = lax.all_gather(pass_attn, "tp", axis=2, tiled=True).reshape(blocks * plen, width)
    query_full, pos_full = (
        lax.all_gather(q_attn, "tp", axis=2, tiled=True),
        lax.all_gather(p_attn, "tp", axis=2, tiled=True),
    )
    query_full = query_full.reshape(queries * qlen, width)
    pos_full = pos_full.reshape(queries * poslen, width)
    proj_s = add_block(pass_full, lax.all_gather(w_snap, "grp", axis=0, tiled=True))
    piece = lax.all_gather(w_out, "grp", axis=0, tiled=True)
    proj_q = add_block(query_full, piece)
    proj_p = add_block(pos_full, piece)
    hidden_s = pass_resid.reshape(blocks * plen, cols).astype(jnp.float32) + proj_s
    squares_s = lax.psum(jnp.sum(hidden_s * hidden_s, axis=1), "tp")
    factor_s, out_s = token_norm(hidden_s, squares_s, width, gain)
    mask = (lax.broadcasted_iota(jnp.int32, (blocks, plen), 1) < pass_len[:, None]).astype(
        jnp.float32
    )
    pooled_s = jnp.sum(out_s.reshape(blocks, plen, cols) * mask[:, :, None], axis=1) / pass_len[
        :, None
    ].astype(jnp.float32)
    pool_sq = lax.psum(jnp.sum(pooled_s * pooled_s, axis=1), "tp")
    passage_index = (pooled_s * lax.rsqrt(pool_sq[:, None] / width + EPS)).astype(jnp.bfloat16)
    hidden_q = q_resid.reshape(queries * qlen, cols).astype(jnp.float32) + proj_q
    hidden_p = p_resid.reshape(queries * poslen, cols).astype(jnp.float32) + proj_p
    squares_q, squares_p = lax.psum(
        (jnp.sum(hidden_q * hidden_q, axis=1), jnp.sum(hidden_p * hidden_p, axis=1)), "tp"
    )
    factor_q, out_q = token_norm(hidden_q, squares_q, width, gain)
    factor_p, out_p = token_norm(hidden_p, squares_p, width, gain)
    pooled_q = jnp.mean(out_q.reshape(queries, qlen, cols), axis=1)
    pooled_p = jnp.mean(out_p.reshape(queries, poslen, cols), axis=1)
    index_all = lax.all_gather(passage_index, "grp", axis=0, tiled=True)
    owners = block_owner.shape[0]
    match = (neg_ids // blocks)[:, :, None] == lax.broadcasted_iota(jnp.int32, (1, 1, owners), 2)
    owner_of = jnp.sum(jnp.where(match, block_owner[None, None, :], 0), axis=2)
    slots = owner_of * blocks + neg_ids % blocks
    neg_rows = index_all[slots].astype(jnp.float32)
    sq_q, sq_p = lax.psum(
        (jnp.sum(pooled_q * pooled_q, axis=1), jnp.sum(pooled_p * pooled_p, axis=1)), "tp"
    )
    norm_q = lax.rsqrt(sq_q / width + EPS)
    norm_p = lax.rsqrt(sq_p / width + EPS)
    emb_q = pooled_q * norm_q[:, None]
    emb_p = pooled_p * norm_p[:, None]
    pos, neg = lax.psum(
        (
            jnp.sum(emb_q * emb_p, axis=1),
            jnp.einsum("qc,qjc->qj", emb_q, neg_rows, precision=precise),
        ),
        "tp",
    )
    scale = 1.0 / (width * TEMP)
    exp_pos = jnp.exp(pos * scale)
    exp_neg = jnp.exp(neg * scale)
    total = exp_pos + jnp.sum(exp_neg, axis=1)
    terms = jnp.log(total) - pos * scale
    loss = lax.psum(jnp.sum(terms), "grp") / (queries * grp_size)
    d_pos = exp_pos / total - 1.0
    d_neg = exp_neg / total[:, None]
    grad_q = (
        d_pos[:, None] * emb_p + jnp.einsum("qj,qjc->qc", d_neg, neg_rows, precision=precise)
    ) * scale
    grad_p = d_pos[:, None] * emb_q * scale
    back_q, back_p = lax.psum(
        (jnp.sum(emb_q * grad_q, axis=1), jnp.sum(emb_p * grad_p, axis=1)), "tp"
    )
    seq_q = norm_q[:, None] * (grad_q - emb_q * back_q[:, None] / width)
    seq_p = norm_p[:, None] * (grad_p - emb_p * back_p[:, None] / width)
    upper_q = spread_tokens(seq_q / qlen * gain[None, :], qlen)
    upper_p = spread_tokens(seq_p / poslen * gain[None, :], poslen)
    normed_q = hidden_q * factor_q
    normed_p = hidden_p * factor_p
    inner_q, inner_p = lax.psum(
        (jnp.sum(normed_q * upper_q, axis=1), jnp.sum(normed_p * upper_p, axis=1)), "tp"
    )
    dh_q = (factor_q * (upper_q - normed_q * inner_q[:, None] / width)).astype(jnp.bfloat16)
    dh_p = (factor_p * (upper_p - normed_p * inner_p[:, None] / width)).astype(jnp.bfloat16)
    w_grad = lax.psum_scatter(
        contract_rows(query_full, dh_q) + contract_rows(pos_full, dh_p),
        "grp",
        scatter_dimension=0,
        tiled=True,
    )
    return (loss, w_grad, passage_index)


def solution(mesh):
    placed = (
        P("grp", None, "tp"),
        P("grp", None, "tp"),
        P("grp", None, "tp"),
        P("grp", None, "tp"),
        P("grp", "tp"),
        P("grp", "tp"),
        P("tp"),
        P("grp", None, "tp"),
        P("grp", None, "tp"),
        P("grp"),
        P(),
        P("grp", None),
    )
    return jax.shard_map(
        shards,
        mesh=mesh,
        in_specs=placed,
        out_specs=(P(), P("grp", "tp"), P("grp", "tp")),
        check_vma=False,
    )
```

profile of v0, /device:TPU:2, one launch (start us, length us, event | category | flops | bytes accessed | tf_op | source)
XLA Modules:
  0.0 730.8 jit_solution(12068333558267169497)
XLA Ops:
  7.2 0.0 copy-start.3
  7.2 0.0 all-gather.7.cloned.1.call-start
  7.2 0.7 all-gather.7.cloned.1.call-update
  7.9 0.0 all-gather.9.cloned.1.call-start
  8.0 0.7 all-gather.9.cloned.1.call-update
  8.7 0.0 all-gather.11.cloned.1.call-start
  8.7 0.7 all-gather.11.cloned.1.call-update
  9.4 0.0 all-gather.13.cloned.1.call-start
  9.4 0.5 all-gather.13.cloned.1.call-update
  10.0 0.0 all-gather.15.cloned.1.call-start
  10.0 0.5 all-gather.15.cloned.1.call-update
  10.6 0.0 reduce-scatter.2.cloned.1.call-start
  10.6 0.7 convert_element_type.44
  11.3 0.7 convert_element_type.50
  11.9 0.7 and_select_fusion.1
  12.6 0.9 select_reduce_fusion
  13.5 0.7 compare_select_fusion
  14.2 0.1 reshape.170
  14.3 0.7 compare_convert_fusion
  15.0 0.7 broadcast_multiply_fusion.2
  15.7 59.5 %all-gather.7.cloned.1.call-done = bf16[2,64,4096]{2,1,0:T(8,128)(2,1)} async-done(((bf16[2,64,512]{2,1,0:T(8,128)(2,1)}), bf16[2,64,4096]{2,1,0:T(8,128)(2,1)}) %all-gather.7.cloned.1.call-update) | async-done | bytes 1048592 | tf_op jit(solution)/shard_map/all_gather | solution.py:53
  75.2 60.2 %all-gather.9.cloned.1.call-done = bf16[4096,512]{1,0:T(8,128)(2,1)} async-done(((bf16[128,512]{1,0:T(8,128)(2,1)}), bf16[4096,512]{1,0:T(8,128)(2,1)}) %all-gather.9.cloned.1.call-update) | async-done | bytes 4194320 | tf_op jit(solution)/shard_map/all_gather | solution.py:59
  135.3 3.3 multiply_reduce_fusion.3
  138.6 0.0 copy-start.2
  138.6 75.1 %all-gather.11.cloned.1.call-done = bf16[2,128,4096]{2,1,0:T(8,128)(2,1)} async-done(((bf16[2,128,512]{2,1,0:T(8,128)(2,1)}), bf16[2,128,4096]{2,1,0:T(8,128)(2,1)}) %all-gather.11.cloned.1.call-update) | async-done | bytes 2097168 | tf_op jit(solution)/shard_map/all_gather | solution.py:54
  213.7 4.1 multiply_reduce_fusion.2
  217.9 105.9 %all-gather.13.cloned.1.call-done = bf16[2,256,4096]{2,1,0:T(8,128)(2,1)} async-done(((bf16[2,256,512]{2,1,0:T(8,128)(2,1)}), bf16[2,256,4096]{2,1,0:T(8,128)(2,1)}) %all-gather.13.cloned.1.call-update) | async-done | bytes 4194320 | tf_op jit(solution)/shard_map/all_gather | solution.py:51
  323.8 60.0 %all-gather.15.cloned.1.call-done = bf16[4096,512]{1,0:T(8,128)(2,1)} async-done(((bf16[128,512]{1,0:T(8,128)(2,1)}), bf16[4096,512]{1,0:T(8,128)(2,1)}) %all-gather.15.cloned.1.call-update) | async-done | bytes 4194320 | tf_op jit(solution)/shard_map/all_gather | solution.py:58
  383.8 5.9 multiply_reduce_fusion.1
  389.7 30.2 %all-reduce.4 = (f32[256]{0:T(256)S(1)}, f32[128]{0:T(128)S(1)}, f32[512]{0:T(512)S(1)}) all-reduce(f32[256]{0:T(256)S(1)} %get-tuple-element.42, f32[128]{0:T(128)S(1)} %get-tuple-element.44, f32[512]{0:T(512)S(1)} %get-tuple-element.46), channel_id=1, replica_groups=mesh['grp'=32,'tp'=8] {'tp'}, use_global_device_ids=true, to_apply=%region_6.0 | all-reduce | flops 896 | bytes 7168 | tf_op jit(solution)/shard_map/psum | solution.py:75
  419.9 0.1 bitcast_reduce_fusion
  420.0 0.1 multiply_reduce_fusion.8
  420.2 0.1 bitcast_reduce_fusion.1
  420.3 0.1 multiply_reduce_fusion.9
  420.4 0.2 multiply_reduce_fusion
  420.6 0.2 multiply_reduce_fusion.6
  420.8 23.9 %all-reduce.3 = (f32[2]{0:T(128)S(1)}, f32[2]{0:T(128)S(1)}, f32[2]{0:T(128)S(1)}) all-reduce(f32[2]{0:T(128)S(1)} %multiply_reduce_fusion.8, f32[2]{0:T(128)S(1)} %multiply_reduce_fusion.9, f32[2]{0:T(128)S(1)} %get-tuple-element.27), channel_id=1, replica_groups=mesh['grp'=32,'tp'=8] {'tp'}, use_global_device_ids=true, to_apply=%region_9.0 | all-reduce | flops 6 | bytes 48 | tf_op jit(solution)/shard_map/psum | solution.py:88
  444.7 0.1 fusion.29
  444.8 38.9 %all-gather = bf16[32,2,512]{2,1,0:T(2,128)(2,1)S(1)} all-gather(bf16[1,2,512]{2,1,0:T(2,128)(2,1)S(1)} %fusion.29), channel_id=1, replica_groups=mesh['grp'=32,'tp'=8] {'grp'}, dimensions={0}, use_global_device_ids=true | all-gather | bytes 67584 | tf_op jit(solution)/shard_map/all_gather | solution.py:82
  483.7 0.6 gather_fusion
  484.3 0.2 fusion.15
  484.4 0.1 fusion.6
  484.6 29.8 %all-reduce.2 = (f32[2]{0:T(128)S(1)}, f32[2,8]{1,0:T(2,128)S(1)}) all-reduce(f32[2]{0:T(128)S(1)} %get-tuple-element.32, f32[2,8]{1,0:T(2,128)S(1)} %bitcast.74), channel_id=1, replica_groups=mesh['grp'=32,'tp'=8] {'tp'}, use_global_device_ids=true, to_apply=%region_11.12 | all-reduce | flops 18 | bytes 144 | tf_op jit(solution)/shard_map/psum | solution.py:95
  514.3 0.1 fusion.14
  514.5 0.6 exponential_add_fusion
  515.1 0.1 fusion.13
  515.1 0.1 fusion.8
  515.3 0.2 multiply_reduce_fusion.4
  515.5 23.9 %all-reduce.1 = (f32[2]{0:T(128)S(1)}, f32[2]{0:T(128)S(1)}) all-reduce(f32[2]{0:T(128)S(1)} %get-tuple-element.13, f32[2]{0:T(128)S(1)} %get-tuple-element.12), channel_id=1, replica_groups=mesh['grp'=32,'tp'=8] {'tp'}, use_global_device_ids=true, to_apply=%region_23.24 | all-reduce | flops 4 | bytes 32 | tf_op jit(solution)/shard_map/psum | solution.py:114
  539.3 0.1 multiply_multiply_fusion.3
  539.4 0.2 fusion
  539.6 0.2 fusion.3
  539.8 29.8 %all-reduce = (f32[128]{0:T(128)S(1)}, f32[256]{0:T(256)S(1)}) all-reduce(f32[128]{0:T(128)S(1)} %fusion.3, f32[256]{0:T(256)S(1)} %fusion), channel_id=1, replica_groups=mesh['grp'=32,'tp'=8] {'tp'}, use_global_device_ids=true, to_apply=%region_25.26 | all-reduce | flops 384 | bytes 3072 | tf_op jit(solution)/shard_map/psum | solution.py:123
  569.6 0.1 fusion.5
  569.7 0.0 copy-done
  569.7 1.3 fusion.17
  571.0 0.2 fusion.2
  571.2 0.1 copy-done.1
  571.3 4.5 add_bitcast_fusion
  575.8 0.0 reduce-scatter.2.cloned.1.call-update
  575.9 64.9 %psum.99 = f32[]{:T(128)} all-reduce(f32[]{:T(128)} %get-tuple-element.36), channel_id=1, replica_groups=mesh['grp'=32,'tp'=8] {'grp'}, use_global_device_ids=true, to_apply=%region_21.22 | all-reduce | flops 1 | bytes 8 | tf_op jit(solution)/shard_map/psum | solution.py:107
  641.4 0.7 multiply_convert_fusion
  642.1 78.9 %reduce-scatter.2.cloned.1.call-done = f32[128,512]{0,1:T(8,128)} async-done(((f32[4096,512]{0,1:T(8,128)}), f32[128,512]{0,1:T(8,128)}) %reduce-scatter.2.cloned.1.call-update) | async-done | bytes 262160 | tf_op jit(solution)/shard_map/reduce_scatter | solution.py:128
  721.0 1.8 copy.17
  (11 shorter events, 0.1 us)
Async XLA Ops:
  7.2 206.6 %copy-start.3 = (bf16[2,128,512]{2,1,0:T(8,128)(2,1)S(1)}, bf16[2,128,512]{2,1,0:T(8,128)(2,1)}, u32[]{:S(2)}) copy-start(bf16[2,128,512]{2,1,0:T(8,128)(2,1)} %param.15) | copy-start | bytes 786436
  7.2 68.0 %all-gather.7.cloned.1.call-start = ((), (), s32[]{:S(2)}) async-start(), calls=%async_computation.1 | async-start | bytes 1179648 | tf_op jit(solution)/shard_map/all_gather | solution.py:53
  7.9 127.4 %all-gather.9.cloned.1.call-start = ((), (), s32[]{:S(2)}) async-start(), calls=%async_computation.2 | async-start | bytes 4325376 | tf_op jit(solution)/shard_map/all_gather | solution.py:59
  8.7 205.1 %all-gather.11.cloned.1.call-start = ((), (), s32[]{:S(2)}) async-start(), calls=%async_computation.3 | async-start | bytes 2359296 | tf_op jit(solution)/shard_map/all_gather | solution.py:54
  9.4 314.4 %all-gather.13.cloned.1.call-start = ((), (), s32[]{:S(2)}) async-start(), calls=%async_computation.4 | async-start | bytes 4718592 | tf_op jit(solution)/shard_map/all_gather | solution.py:51
  10.0 373.8 %all-gather.15.cloned.1.call-start = ((), (), s32[]{:S(2)}) async-start(), calls=%async_computation.5 | async-start | bytes 4325376 | tf_op jit(solution)/shard_map/all_gather | solution.py:58
  10.6 710.5 %reduce-scatter.2.cloned.1.call-start = ((), (), s32[]{:S(2)}) async-start(), calls=%async_computation.6 | async-start | bytes 8650752 | tf_op jit(solution)/shard_map/reduce_scatter | solution.py:128
  138.6 245.2 %copy-start.2 = (bf16[2,256,512]{2,1,0:T(8,128)(2,1)S(1)}, bf16[2,256,512]{2,1,0:T(8,128)(2,1)}, u32[]{:S(2)}) copy-start(bf16[2,256,512]{2,1,0:T(8,128)(2,1)} %param.20) | copy-start | bytes 1572868
  389.7 180.0 %copy-start = (bf16[2,64,4096]{2,1,0:T(8,128)(2,1)S(1)}, bf16[2,64,4096]{2,1,0:T(8,128)(2,1)}, u32[]{:S(2)}) copy-start(bf16[2,64,4096]{2,1,0:T(8,128)(2,1)} %all-gather.7.cloned.1.call-done) | copy-start | bytes 3145732
  569.7 1.6 copy-start.1
Sparse Core Ops, SparseCore 0:
  10.5 64.6 all-gather.6
  77.0 58.2 all-gather.8
  137.8 75.8 all-gather.10
  216.1 107.6 all-gather.12
  325.5 58.2 all-gather.14
  576.0 145.0 reduce-scatter.1
where the time goes:
time: 737 us; the launch traced here: 731 us
  waiting for transfers between devices  443 us (60%)
  blocking collectives  241 us (33%)
  matrix products  19.4 us (3%)
  between operations  16 us (2%)
  other arithmetic  8.61 us (1%)
    all_gather x1, waiting for transfers between devices, shards(): lax.all_gather(pass_attn, 'tp', axis=2, tiled=True)  106 us
    reduce_scatter x1, waiting for transfers between devices, shards(): lax.psum_scatter(contract_rows(query_full, dh_q) + contract_rows(pos_full...  78.9 us
    all_gather x1, waiting for transfers between devices, shards(): lax.all_gather(p_attn, 'tp', axis=2, tiled=True)  75.1 us
    psum x1, blocking collectives, shards(): loss = lax.psum(jnp.sum(terms), 'grp') / (queries * grp_size)  64.9 us
    all_gather x1, waiting for transfers between devices, shards(): piece = lax.all_gather(w_out, 'grp', axis=0, tiled=True)  60.2 us
    all_gather x1, waiting for transfers between devices, shards(): lax.all_gather(w_snap, 'grp', axis=0, tiled=True)  60 us
    all_gather x1, waiting for transfers between devices, shards(): lax.all_gather(q_attn, 'tp', axis=2, tiled=True)  59.5 us
    all_gather x1, blocking collectives, shards(): index_all = lax.all_gather(passage_index, 'grp', axis=0, tiled=True)  38.9 us
  transfers between devices with their start and end apart: 6, of which 6 were waited for; matrix products, arithmetic and copies ran while one was open for 2% of the time, Pallas kernels for 0%

commit v1 on v0

v1 whole, which is shorter than its diff:
```python
import functools

import jax
import jax.numpy as jnp
from jax import lax
from jax.experimental import pallas as pl
from jax.experimental.pallas import tpu as pltpu
from jax.sharding import PartitionSpec as P

EPS = 1e-06
TEMP = 0.05
WIDTH = 4096
COLS = 512
STOK = 512
ETOK = 384
SCALE = 1.0 / (WIDTH * TEMP)
MESH = pl.DeviceIdType.MESH
HI = lax.Precision.HIGHEST
F32 = jnp.float32
BF16 = jnp.bfloat16
HALF = (0, 1, 1, 0, 0, 1)
STEP = (1, 1, -1, -1, 1, -1)


def lanes4(col):
    return jnp.concatenate([col, col, col, col], axis=1)


def spread_rows(row):
    return jnp.broadcast_to(row, (128, 128)).T


def square_rows(h_ref, block):
    part = h_ref[pl.ds(block * 128, 128), :]
    part = part * part
    part = (part[:, 0:128] + part[:, 128:256]) + (part[:, 256:384] + part[:, 384:512])
    return jnp.sum(part.T, axis=0, keepdims=True)


def kernel(
    q_attn, q_resid, p_attn, p_resid, w_out, w_snap, gain_ref, s_attn, s_resid,
    pass_len, block_owner, neg_ids,
    loss_ref, grad_ref, index_ref,
    a_s, a_e, w_s, w_o, r_s, r_e, h_s, h_e, a_t,
    ar_s, ar_p, ar_e, ar_g, ig, pool_s, vec, vec_g, s_full, fcol, gcol, f_row, urow, dh,
    own, psend, precv, xsend, xrecv, zsend, zrecv, l_c, l_x, l_z,
    loc, y_ss, y_rs, z_ss, z_rs, wz_ss, wz_rs, wx_ss, wx_rs, wc_ss, wc_rs,
    ar_ss, ar_rs, ig_ss, ig_rs, pc_ss, pc_rs, px_ss, px_rs, pz_ss, pz_rs, ls_ss, ls_rs,
):
    grp = lax.axis_index("grp")
    t = lax.axis_index("tp")
    core = grp % 2
    x = (grp // 2) % 4
    lo = grp // 8
    y = t // 2
    hi = t % 2
    t_far = y * 2 + (1 - hi)

    def grp_of(l_, x_, c_):
        return (l_ * 8 + x_ * 2 + c_, t)

    def tp_of(y_, h_):
        return (grp, y_ * 2 + h_)

    def remote(src, dst, ss, rs, device):
        return pltpu.make_async_remote_copy(
            src_ref=src, dst_ref=dst, send_sem=ss, recv_sem=rs, device_id=device,
            device_id_type=MESH,
        )

    locals_ = [
        pltpu.make_async_copy(w_snap, w_s.at[grp], loc.at[0]),
        pltpu.make_async_copy(s_attn, a_s.at[t], loc.at[1]),
        pltpu.make_async_copy(w_out, w_o.at[grp], loc.at[2]),
        pltpu.make_async_copy(q_attn, a_e.at[t, pl.ds(0, 128)], loc.at[3]),
        pltpu.make_async_copy(p_attn, a_e.at[t, pl.ds(128, 256)], loc.at[4]),
        pltpu.make_async_copy(s_resid, r_s, loc.at[5]),
        pltpu.make_async_copy(q_resid, r_e.at[pl.ds(0, 128)], loc.at[6]),
        pltpu.make_async_copy(p_resid, r_e.at[pl.ds(128, 256)], loc.at[7]),
    ]
    for copy in locals_:
        copy.start()

    barrier = pltpu.get_barrier_semaphore()
    peers = [grp_of(lo, x, 1 - core)]
    for d in (1, 2, 3):
        peers.append(grp_of(lo, (x + d) % 4, core))
        peers.append(grp_of((lo + d) % 4, x, core))
    for j in range(1, 8):
        peers.append(tp_of((y + j // 2) % 4, (hi + j % 2) % 2))
    for peer in peers:
        pl.semaphore_signal(barrier, inc=1, device_id=peer, device_id_type=MESH)
    vec[...] = jnp.zeros_like(vec)
    s_full[...] = jnp.zeros_like(s_full)
    pl.semaphore_wait(barrier, len(peers))

    def y_copy(k, i):
        buf, size = ((a_s, 256), (a_e, 192))[k % 2]
        half_of = hi if k < 2 else 1 - hi
        row = y if i < 4 else (y - STEP[i] + 4) % 4
        ref = buf.at[row * 2 + half_of, pl.ds(HALF[i] * size, size)]
        return remote(
            ref, ref, y_ss.at[k, i], y_rs.at[k, i], tp_of((y + STEP[i] + 4) % 4, hi)
        )

    def y_arrival(k, i):
        buf, size = ((a_s, 256), (a_e, 192))[k % 2]
        half_of = hi if k < 2 else 1 - hi
        row = (y - STEP[i] * (1 if i < 4 else 2) + 4) % 4
        ref = buf.at[row * 2 + half_of, pl.ds(HALF[i] * size, size)]
        return remote(ref, ref, y_ss.at[k, i], y_rs.at[k, i], tp_of(y, hi))

    def far_copy(k, half, slot):
        buf, size = ((a_s, 256), (a_e, 192))[k]
        ref = buf.at[slot, pl.ds(half * size, size)]
        return remote(ref, ref, z_ss.at[k, half], z_rs.at[k, half], tp_of(y, 1 - hi))

    weights = (w_s, w_o)

    def wz_copy(m, d, source):
        ref = weights[m].at[source * 8 + x * 2 + core]
        return remote(
            ref, ref, wz_ss.at[m, d], wz_rs.at[m, d], grp_of((lo + d) % 4, x, core)
        )

    def wx_copy(m, b, d, x_):
        ref = weights[m].at[((lo - b + 4) % 4) * 8 + x_ * 2 + core]
        return remote(
            ref, ref, wx_ss.at[m, b, d], wx_rs.at[m, b, d], grp_of(lo, (x + d) % 4, core)
        )

    def wc_copy(m, b, d, c_):
        ref = weights[m].at[((lo - b + 4) % 4) * 8 + ((x - d + 4) % 4) * 2 + c_]
        return remote(
            ref, ref, wc_ss.at[m, b, d], wc_rs.at[m, b, d], grp_of(lo, x, 1 - core)
        )

    def w_spread(m, b):
        for d in (2, 1, 3):
            wx_copy(m, b, d, x).start()
        wc_copy(m, b, 0, core).start()

    def ar_copy(which, buf, j, slot):
        ref = buf.at[slot]
        return remote(
            ref, ref, ar_ss.at[which, j], ar_rs.at[which, j],
            tp_of((y + j // 2) % 4, (hi + j % 2) % 2),
        )

    def ar_start(which, buf):
        for j in (5, 7, 3, 4, 1, 2, 6):
            ar_copy(which, buf, j, t).start()

    def ar_finish(which, buf):
        for j in range(1, 8):
            ar_copy(which, buf, j, ((y - j // 2 + 4) % 4) * 2 + (hi + j % 2) % 2).wait_recv()
        total = buf[0]
        for j in range(1, 8):
            total = total + buf[j]
        return total

    def ig_copy(i, l_, x_, c_):
        if i == 0:
            ref, device = ig.at[lo, x * 2 + c_], grp_of(lo, x, 1 - core)
        elif i < 4:
            ref, device = ig.at[lo, pl.ds(x_ * 2, 2)], grp_of(lo, (x + i) % 4, core)
        else:
            ref, device = ig.at[l_], grp_of((lo + i - 3) % 4, x, core)
        return remote(ref, ref, ig_ss.at[i], ig_rs.at[i], device)

    def multiply(h_ref, buf, w_ref, half_of):
        def body(i, carry):
            k = ((y + i) % 4) * 2 + half_of
            piece = w_ref[pl.ds(4 * k, 4)].reshape(512, COLS)
            h_ref[...] += jnp.dot(buf[k], piece, preferred_element_type=F32)
            return carry

        lax.fori_loop(0, 4, body, 0)

    def turn(half_of):
        def body(i, carry):
            k = ((y + i) % 4) * 2 + half_of
            a_t[pl.ds(k * 512, 512), :] = a_e[k].T
            return carry

        lax.fori_loop(0, 4, body, 0)

    for i in (0, 1):
        locals_[i].wait()
    for d in (2, 1, 3):
        wz_copy(0, d, lo).start()
    w_spread(0, 0)
    for i in range(4):
        y_copy(0, i).start()
    for half in (0, 1):
        far_copy(0, half, t).start()
    for i in (2, 3, 4):
        locals_[i].wait()
    for d in (2, 1, 3):
        wz_copy(1, d, lo).start()
    w_spread(1, 0)
    for i in range(4):
        y_copy(1, i).start()
    for half in (0, 1):
        far_copy(1, half, t).start()
    for i in (5, 6, 7):
        locals_[i].wait()
    h_s[...] = r_s[...].astype(F32)
    h_e[...] = r_e[...].astype(F32)

    for b in (1, 3, 2):
        wz_copy(0, b, (lo - b + 4) % 4).wait_recv()
        w_spread(0, b)
    for i in (0, 2):
        y_arrival(0, i).wait_recv()
        y_copy(0, 4 + i // 2).start()
    for b in (1, 3, 2):
        wz_copy(1, b, (lo - b + 4) % 4).wait_recv()
        w_spread(1, b)
    for i in (0, 2):
        y_arrival(1, i).wait_recv()
        y_copy(1, 4 + i // 2).start()
    for half in (0, 1):
        far_copy(0, half, t_far).wait_recv()
    for i in range(4):
        y_copy(2, i).start()
    for b in (0, 1, 3, 2):
        for d in (1, 3, 2):
            wx_copy(0, b, d, (x - d + 4) % 4).wait_recv()
            wc_copy(0, b, d, core).start()
    for i in (0, 2):
        y_arrival(2, i).wait_recv()
        y_copy(2, 4 + i // 2).start()
    for b in range(4):
        for d in range(4):
            wc_copy(0, b, d, 1 - core).wait_recv()
    for i in (1, 3, 4, 5):
        y_arrival(0, i).wait_recv()
    multiply(h_s, a_s, w_s, hi)
    for half in (0, 1):
        far_copy(1, half, t_far).wait_recv()
    for i in range(4):
        y_copy(3, i).start()
    for i in (1, 3, 4, 5):
        y_arrival(1, i).wait_recv()
    turn(hi)
    for b in (0, 1, 3, 2):
        for d in (1, 3, 2):
            wx_copy(1, b, d, (x - d + 4) % 4).wait_recv()
            wc_copy(1, b, d, core).start()
    for i in (1, 3, 4, 5):
        y_arrival(2, i).wait_recv()
    multiply(h_s, a_s, w_s, 1 - hi)

    ar_s[t] = jnp.zeros((8, 128), F32)
    for b in range(4):
        ar_s[t, b : b + 1, :] = square_rows(h_s, b)
    ar_start(0, ar_s)
    for i in (0, 2):
        y_arrival(3, i).wait_recv()
        y_copy(3, 4 + i // 2).start()
    for b in range(4):
        for d in range(4):
            wc_copy(1, b, d, 1 - core).wait_recv()
    multiply(h_e, a_e, w_o, hi)
    gain = gain_ref[...].astype(F32)

    factor_s = lax.rsqrt(ar_finish(0, ar_s) / WIDTH + EPS)
    ar_p[t] = jnp.zeros((8, 128), F32)
    for s in range(2):
        count = pass_len[s]
        total = jnp.zeros((1, COLS), F32)
        for b in range(2):
            rows = lax.broadcasted_iota(jnp.int32, (128, 128), 0) + b * 128
            col = spread_rows(factor_s[2 * s + b : 2 * s + b + 1, :])
            col = jnp.where(rows < count, col, 0.0)
            part = h_s[pl.ds((2 * s + b) * 128, 128), :] * lanes4(col)
            total = total + jnp.sum(part, axis=0, keepdims=True)
        total = total * gain / jnp.full((1, COLS), count, jnp.int32).astype(F32)
        pool_s[s : s + 1, :] = total
        square = jnp.sum(total * total, axis=1, keepdims=True)
        ar_p[t, s : s + 1, :] = jnp.broadcast_to(square, (1, 128))
    ar_start(1, ar_p)
    norm_s = lax.rsqrt(ar_finish(1, ar_p) / WIDTH + EPS)
    for s in range(2):
        row = (pool_s[s : s + 1, :] * lanes4(norm_s[s : s + 1, :])).astype(BF16).astype(F32)
        pool_s[s : s + 1, :] = row
        for b in range(4):
            ig[lo, x * 2 + core, 4 * s + b : 4 * s + b + 1, :] = row[:, b * 128 : b * 128 + 128]
    index_ref[...] = pool_s[0:2, :].astype(BF16)
    ig_copy(0, lo, x, core).start()
    ig_copy(0, lo, x, 1 - core).wait_recv()
    for i in (2, 1, 3):
        ig_copy(i, lo, x, core).start()

    for i in (1, 3, 4, 5):
        y_arrival(3, i).wait_recv()
    multiply(h_e, a_e, w_o, 1 - hi)
    ar_e[t] = jnp.zeros((8, 128), F32)
    for b in range(3):
        ar_e[t, b : b + 1, :] = square_rows(h_e, b)
    ar_start(2, ar_e)
    for i in (1, 2, 3):
        ig_copy(i, lo, (x - i + 4) % 4, core).wait_recv()
    for i in (5, 4, 6):
        ig_copy(i, lo, x, core).start()
    turn(1 - hi)

    factor = lax.rsqrt(ar_finish(2, ar_e) / WIDTH + EPS)
    f_row[...] = factor
    for b in range(3):
        fcol[pl.ds(b * 128, 128), :] = spread_rows(factor[b : b + 1, :])
    for r, (first, count) in enumerate(((0, 64), (64, 64), (128, 128), (256, 128))):
        part = h_e[pl.ds(first, count), :] * lanes4(fcol[pl.ds(first, count), :])
        vec[r : r + 1, :] = jnp.sum(part, axis=0, keepdims=True) * gain / count
    for i in (4, 5, 6):
        ig_copy(i, (lo - i + 3 + 4) % 4, x, core).wait_recv()
    for r in range(2):
        for j in range(8):
            name = neg_ids[r, j]
            owner = block_owner[name // 2]
            tile = ig[owner // 8, owner % 8]
            piece = jnp.where(name % 2 == 0, tile[0:4, :], tile[4:8, :])
            at = 8 + 8 * r + j
            for b in range(4):
                vec[at : at + 1, b * 128 : b * 128 + 128] = piece[b : b + 1, :]

    nt = (((1,), (1,)), ((), ()))
    vec_g[...] = vec[0:32, :] * gain
    sims = lax.dot_general(vec_g[...], h_e[...], nt, precision=HI, preferred_element_type=F32)
    gram = lax.dot_general(vec[0:8, :], vec[...], nt, precision=HI, preferred_element_type=F32)
    first = lax.broadcasted_iota(jnp.int32, (1, 128), 1) < 64
    ar_g[t, 0:8, :] = jnp.where(first, sims[8:16, 0:128], sims[16:24, 0:128])
    ar_g[t, 8:16, :] = jnp.zeros((8, 128), F32)
    ar_g[t, 8:9, :] = jnp.where(first, sims[0:1, 0:128], sims[1:2, 0:128])
    ar_g[t, 9:10, :] = jnp.where(first, sims[2:3, 0:128], sims[3:4, 0:128])
    ar_g[t, 10:11, :] = sims[0:1, 128:256]
    ar_g[t, 11:12, :] = sims[2:3, 128:256]
    ar_g[t, 12:13, :] = sims[1:2, 256:384]
    ar_g[t, 13:14, :] = sims[3:4, 256:384]
    ar_g[t, 16:24, :] = gram
    ar_start(3, ar_g)
    both = ar_finish(3, ar_g)

    gram = both[16:24, :]
    row = lax.broadcasted_iota(jnp.int32, (8, 128), 0)
    lane = lax.broadcasted_iota(jnp.int32, (8, 128), 1)
    diag = jnp.where((lane == row) & (row < 4), gram, 0.0)
    norm_row = lax.rsqrt(jnp.sum(diag, axis=1, keepdims=True) / WIDTH + EPS)
    norm_lane = lax.rsqrt(jnp.sum(diag, axis=0, keepdims=True) / WIDTH + EPS)
    norm_lane = jnp.where(lane < 4, norm_lane, 1.0)
    unit = gram * norm_row * norm_lane
    is_pos = (lane == row + 2) & (row < 2)
    is_neg = (lane >= 8 + 8 * row) & (lane < 16 + 8 * row) & (row < 2)
    pos = jnp.sum(jnp.where(is_pos, unit, 0.0), axis=1, keepdims=True) * SCALE
    exp_neg = jnp.where(is_neg, jnp.exp(jnp.where(is_neg, unit, 0.0) * SCALE), 0.0)
    exp_pos = jnp.exp(pos)
    total = exp_pos + jnp.sum(exp_neg, axis=1, keepdims=True)
    terms = jnp.where(row < 2, jnp.log(total) - pos, 0.0)
    loss = jnp.sum(terms, axis=0, keepdims=True)
    d_pos = jnp.where(is_pos, exp_pos / total - 1.0, 0.0)
    pos_lane = jnp.sum(d_pos, axis=0, keepdims=True)
    pos_row = jnp.sum(jnp.where(lane == row, pos_lane, 0.0), axis=1, keepdims=True)
    coef = d_pos + exp_neg / total
    coef = coef + jnp.where((lane == row - 2) & (row < 4), pos_row, 0.0)
    coef = coef * SCALE
    back = jnp.sum(coef * unit, axis=1, keepdims=True) / WIDTH
    coef = norm_row * (coef * norm_lane - jnp.where(lane == row, back * norm_row, 0.0))
    coef = jnp.where(row < 4, coef, 0.0)
    coef = coef / jnp.where(row < 2, 64.0, 128.0)

    l_c[core] = jnp.broadcast_to(loss, (8, 128))
    pair_loss = remote(
        l_c.at[core], l_c.at[core], ls_ss.at[0], ls_rs.at[0], grp_of(lo, x, 1 - core)
    )
    pair_loss.start()

    s_full[8:16, 0:128] = both[0:8, :]
    s_full[16:24, 0:128] = both[0:8, :]
    s_full[0:2, 0:128] = jnp.broadcast_to(both[8:9, :], (2, 128))
    s_full[2:4, 0:128] = jnp.broadcast_to(both[9:10, :], (2, 128))
    s_full[0:1, 128:256] = both[10:11, :]
    s_full[2:3, 128:256] = both[11:12, :]
    s_full[1:2, 256:384] = both[12:13, :]
    s_full[3:4, 256:384] = both[13:14, :]
    inner = jnp.dot(coef, s_full[...], precision=HI, preferred_element_type=F32)
    urow[...] = jnp.dot(coef, vec[...], precision=HI, preferred_element_type=F32) * gain
    wanted = (
        ((row == 0) & (lane < 64)) | ((row == 1) & (lane >= 64)),
        row == 2,
        row == 3,
    )
    for b in range(3):
        line = jnp.sum(
            jnp.where(wanted[b], inner[:, b * 128 : b * 128 + 128], 0.0), axis=0, keepdims=True
        )
        f = f_row[b : b + 1, :]
        gcol[pl.ds(b * 128, 128), :] = spread_rows(line * f * f / WIDTH)
    for r, (first, count) in enumerate(((0, 64), (64, 64), (128, 128), (256, 128))):
        at = pl.ds(first, count)
        part = urow[r : r + 1, :] - h_e[at, :] * lanes4(gcol[at, :])
        dh[at, :] = (lanes4(fcol[at, :]) * part).astype(BF16)

    def pc_copy(i, x_):
        return remote(
            psend.at[x_], precv.at[x_], pc_ss.at[i], pc_rs.at[i], grp_of(lo, x, 1 - core)
        )

    def px_copy(i, d, dst):
        return remote(
            xsend.at[i, d], xrecv.at[i, d], px_ss.at[i, d], px_rs.at[i, d], grp_of(lo, dst, core)
        )

    def pz_copy(d):
        return remote(
            zsend.at[d], zrecv.at[d], pz_ss.at[d], pz_rs.at[d], grp_of((lo + d) % 4, x, core)
        )

    turns = (2, 1, 3, 0)
    for i in range(4):
        x_ = (x + turns[i]) % 4

        def other(l_, carry, x_=x_):
            at = pl.ds((l_ * 8 + x_ * 2 + 1 - core) * 128, 128)
            psend[x_, l_] = jnp.dot(
                a_t[at, :], dh[...], preferred_element_type=F32
            ).astype(BF16)
            return carry

        def mine(l_, carry, x_=x_):
            at = pl.ds((l_ * 8 + x_ * 2 + core) * 128, 128)
            own[x_, l_] = jnp.dot(a_t[at, :], dh[...], preferred_element_type=F32)
            return carry

        lax.fori_loop(0, 4, other, 0)
        pc_copy(i, x_).start()
        lax.fori_loop(0, 4, mine, 0)

    pair_loss.wait_recv()
    l_x[x] = l_c[0] + l_c[1]

    def lx_copy(d, slot):
        return remote(
            l_x.at[slot], l_x.at[slot], ls_ss.at[d], ls_rs.at[d], grp_of(lo, (x + d) % 4, core)
        )

    def lz_copy(d, slot):
        return remote(
            l_z.at[slot], l_z.at[slot], ls_ss.at[3 + d], ls_rs.at[3 + d],
            grp_of((lo + d) % 4, x, core),
        )

    for d in (1, 2, 3):
        lx_copy(d, x).start()
    for i in range(3):
        x_ = (x + turns[i]) % 4
        pc_copy(i, x_).wait_recv()
        for d in (2, 1, 3, 0):
            l_ = (lo + d) % 4
            xsend[i, d] = (own[x_, l_] + precv[x_, l_].astype(F32)).astype(BF16)
            px_copy(i, d, x_).start()
    pc_copy(3, x).wait_recv()
    for d in (1, 2, 3):
        lx_copy(d, (x - d + 4) % 4).wait_recv()
    l_z[lo] = (l_x[0] + l_x[1]) + (l_x[2] + l_x[3])
    for d in (1, 2, 3):
        lz_copy(d, lo).start()
    for d in (2, 1, 3, 0):
        l_ = (lo + d) % 4
        total = own[x, l_] + precv[x, l_].astype(F32)
        for i in (1, 2, 0):
            px_copy(i, d, x).wait_recv()
        total = total + (xrecv[0, d].astype(F32) + xrecv[1, d].astype(F32) + xrecv[2, d].astype(F32))
        if d == 0:
            grad_ref[...] = total
        else:
            zsend[d] = total.astype(BF16)
            pz_copy(d).start()
    for d in (1, 2, 3):
        lz_copy(d, (lo - d + 4) % 4).wait_recv()
    loss_ref[...] = ((l_z[0] + l_z[1]) + (l_z[2] + l_z[3]))[0:1, 0:1] / 64.0
    for d in (1, 3, 2):
        pz_copy(d).wait_recv()
    grad_ref[...] += (zrecv[1].astype(F32) + zrecv[2].astype(F32)) + zrecv[3].astype(F32)

    for k in range(4):
        for i in range(6):
            y_copy(k, i).wait_send()
    for k in range(2):
        for half in (0, 1):
            far_copy(k, half, t).wait_send()
        for d in (1, 2, 3):
            wz_copy(k, d, lo).wait_send()
        for b in range(4):
            for d in (1, 2, 3):
                wx_copy(k, b, d, x).wait_send()
            for d in range(4):
                wc_copy(k, b, d, core).wait_send()
    for which, buf in enumerate((ar_s, ar_p, ar_e, ar_g)):
        for j in range(1, 8):
            ar_copy(which, buf, j, t).wait_send()
    for i in range(7):
        ig_copy(i, lo, x, core).wait_send()
    pair_loss.wait_send()
    for d in (1, 2, 3):
        lx_copy(d, x).wait_send()
        lz_copy(d, lo).wait_send()
        pz_copy(d).wait_send()
    for i in range(4):
        pc_copy(i, x).wait_send()
    for i in range(3):
        for d in range(4):
            px_copy(i, d, x).wait_send()


def shards(
    q_attn, q_resid, p_attn, p_resid, w_out, w_snap, norm_gain, pass_attn, pass_resid,
    pass_len, block_owner, neg_ids,
):
    hbm = pl.BlockSpec(memory_space=pl.ANY)
    vmem = pl.BlockSpec(memory_space=pltpu.VMEM)
    smem = pl.BlockSpec(memory_space=pltpu.SMEM)
    dma = pltpu.SemaphoreType.DMA
    loss, grad, index = pl.pallas_call(
        kernel,
        out_shape=(
            jax.ShapeDtypeStruct((1, 1), F32),
            jax.ShapeDtypeStruct((128, COLS), F32),
            jax.ShapeDtypeStruct((2, COLS), BF16),
        ),
        in_specs=[hbm] * 6 + [vmem] + [hbm] * 2 + [smem] * 3,
        out_specs=(vmem, vmem, vmem),
        scratch_shapes=[
            pltpu.VMEM((8, STOK, COLS), BF16),
            pltpu.VMEM((8, ETOK, COLS), BF16),
            pltpu.VMEM((32, 128, COLS), BF16),
            pltpu.VMEM((32, 128, COLS), BF16),
            pltpu.VMEM((STOK, COLS), BF16),
            pltpu.VMEM((ETOK, COLS), BF16),
            pltpu.VMEM((STOK, COLS), F32),
            pltpu.VMEM((ETOK, COLS), F32),
            pltpu.VMEM((WIDTH, ETOK), BF16),
            pltpu.VMEM((8, 8, 128), F32),
            pltpu.VMEM((8, 8, 128), F32),
            pltpu.VMEM((8, 8, 128), F32),
            pltpu.VMEM((8, 24, 128), F32),
            pltpu.VMEM((4, 8, 8, 128), F32),
            pltpu.VMEM((8, COLS), F32),
            pltpu.VMEM((128, COLS), F32),
            pltpu.VMEM((32, COLS), F32),
            pltpu.VMEM((128, ETOK), F32),
            pltpu.VMEM((ETOK, 128), F32),
            pltpu.VMEM((ETOK, 128), F32),
            pltpu.VMEM((8, 128), F32),
            pltpu.VMEM((8, COLS), F32),
            pltpu.VMEM((ETOK, COLS), BF16),
            pltpu.VMEM((4, 4, 128, COLS), F32),
            pltpu.VMEM((4, 4, 128, COLS), BF16),
            pltpu.VMEM((4, 4, 128, COLS), BF16),
            pltpu.VMEM((3, 4, 128, COLS), BF16),
            pltpu.VMEM((3, 4, 128, COLS), BF16),
            pltpu.VMEM((4, 128, COLS), BF16),
            pltpu.VMEM((4, 128, COLS), BF16),
            pltpu.VMEM((2, 8, 128), F32),
            pltpu.VMEM((4, 8, 128), F32),
            pltpu.VMEM((4, 8, 128), F32),
            dma((8,)),
            dma((4, 6)), dma((4, 6)),
            dma((2, 2)), dma((2, 2)),
            dma((2, 4)), dma((2, 4)),
            dma((2, 4, 4)), dma((2, 4, 4)),
            dma((2, 4, 4)), dma((2, 4, 4)),
            dma((4, 8)), dma((4, 8)),
            dma((7,)), dma((7,)),
            dma((4,)), dma((4,)),
            dma((3, 4)), dma((3, 4)),
            dma((4,)), dma((4,)),
            dma((7,)), dma((7,)),
        ],
        compiler_params=pltpu.CompilerParams(
            collective_id=0, has_side_effects=True, vmem_limit_bytes=56 * 2**20
        ),
    )(
        q_attn.reshape(128, COLS),
        q_resid.reshape(128, COLS),
        p_attn.reshape(256, COLS),
        p_resid.reshape(256, COLS),
        w_out,
        w_snap,
        norm_gain.reshape(1, COLS),
        pass_attn.reshape(STOK, COLS),
        pass_resid.reshape(STOK, COLS),
        pass_len,
        block_owner,
        neg_ids,
    )
    return (loss[0, 0], grad, index)


def solution(mesh):
    placed = (
        P("grp", None, "tp"),
        P("grp", None, "tp"),
        P("grp", None, "tp"),
        P("grp", None, "tp"),
        P("grp", "tp"),
        P("grp", "tp"),
        P("tp"),
        P("grp", None, "tp"),
        P("grp", None, "tp"),
        P("grp"),
        P(),
        P("grp", None),
    )
    return jax.shard_map(
        shards,
        mesh=mesh,
        in_specs=placed,
        out_specs=(P(), P("grp", "tp"), P("grp", "tp")),
        check_vma=False,
    )
```

time: 737 us -> 176 us (0.24)
  waiting for transfers between devices: 443 us -> 0 us
  blocking collectives: 241 us -> 0 us
  Pallas kernels: 0 us -> 169 us
  matrix products: 19.4 us -> 0 us
  between operations: 16 us -> 2.47 us
  other arithmetic: 8.61 us -> 0 us
    all_gather x5 -> x0, waiting for transfers between devices: 361 us -> none  [the longest x1 106 us: shards(): lax.all_gather(pass_attn, 'tp', axis=2, tiled=True)]
    psum x6 -> x0, blocking collectives: 202 us -> none  [the longest x1 64.9 us: shards(): loss = lax.psum(jnp.sum(terms), 'grp') / (queries * grp_size)]
    pallas_call x0 -> x1, Pallas kernels: none -> 169 us  [shards(): pl.pallas_call(kernel, out_shape=(jax.ShapeDtypeStruct((1, 1), F32), jax....]
    reduce_scatter x1 -> x0, waiting for transfers between devices: 78.9 us -> none  [shards(): lax.psum_scatter(contract_rows(query_full, dh_q) + contract_rows(pos_full...]
    all_gather x1 -> x0, blocking collectives: 38.9 us -> none  [shards(): index_all = lax.all_gather(passage_index, 'grp', axis=0, tiled=True)]
    dot_general x7 -> x0, matrix products: 19.4 us -> none  [the longest x3 13.3 us: add_block(): return jnp.dot(tokens, piece, preferred_element_type=jnp.float32)]
  transfers between devices with their start and end apart: 6 -> 0, of which waited for: 6 -> 0; matrix products, arithmetic and copies ran while one was open for 2% -> 0% of each run, Pallas kernels for 0% -> 0%
where the time goes in v1:
time: 176 us; the launch traced here: 175 us
  Pallas kernels  169 us (96%)
  local copies, waits for them, and re-layouts  3.51 us (2%)
  between operations  2.47 us (1%)
    pallas_call x1, Pallas kernels, shards(): pl.pallas_call(kernel, out_shape=(jax.ShapeDtypeStruct((1, 1), F32), jax....  169 us

profile of v1, /device:TPU:2, one launch (start us, length us, event | category | flops | bytes accessed | tf_op | source)
XLA Modules:
  0.0 174.9 jit_solution(5533786527393406086)
XLA Ops:
  0.6 0.0 copy-start.1
  0.6 0.7 copy-done.1
  1.3 0.6 reshape.31.gain_ref
  1.9 168.9 %shard_map.139 = (f32[1,1]{1,0:T(1,128)}, f32[128,512]{1,0:T(8,128)}, bf16[2,512]{1,0:T(2,128)(2,1)}) custom-call(bf16[128,512]{1,0:T(8,128)(2,1)} %bitcast.11, bf16[128,512]{1,0:T(8,128)(2,1)} %bitcast.12, bf16[256,512]{1,0:T(8,128)(2,1)} %bitcast.9, bf16[256,512]{1,0:T(8,128)(2,1)} %bitcast.10, bf16[128,512]{1,0:T(8,128)(2,1)} %w_out.1, ...), custom_call_target="tpu_custom_call" | custom-call | tf_op jit(solution)/shard_map/pallas_call | solution.py:524
  171.5 0.0 copy-start
  171.5 1.7 copy.19
  173.2 0.0 copy-done
  173.2 0.6 copy.20
Async XLA Ops:
  0.6 0.7 copy-start.1
  171.5 1.7 copy-start

commit v2 on v1

--- a/solution.py
+++ b/solution.py
@@ -22,6 +22,33 @@
 STEP = (1, 1, -1, -1, 1, -1)
 
 
+class Copy:
+    def __init__(self, sent, src, dst, sems, at, device):
+        self.sent = sent
+        self.key = (id(sems), at)
+        self.copy = pltpu.make_async_remote_copy(
+            src_ref=src, dst_ref=dst, send_sem=sems[0].at[at], recv_sem=sems[1].at[at],
+            device_id=device, device_id_type=MESH,
+        )
+
+    def start(self, when=None):
+        self.when = when
+        self.sent.append(self)
+        self.guard(when, self.copy.start)
+
+    def wait_recv(self, when=None):
+        self.guard(when, self.copy.wait_recv)
+
+    def wait_send(self):
+        self.guard(self.when, self.copy.wait_send)
+
+    def guard(self, when, action):
+        if when is None:
+            action()
+        else:
+            pl.when(when)(action)
+
+
 def lanes4(col):
     return jnp.concatenate([col, col, col, col], axis=1)
 
@@ -44,8 +71,8 @@
     a_s, a_e, w_s, w_o, r_s, r_e, h_s, h_e, a_t,
     ar_s, ar_p, ar_e, ar_g, ig, pool_s, vec, vec_g, s_full, fcol, gcol, f_row, urow, dh,
     own, psend, precv, xsend, xrecv, zsend, zrecv, l_c, l_x, l_z,
-    loc, y_ss, y_rs, z_ss, z_rs, wz_ss, wz_rs, wx_ss, wx_rs, wc_ss, wc_rs,
-    ar_ss, ar_rs, ig_ss, ig_rs, pc_ss, pc_rs, px_ss, px_rs, pz_ss, pz_rs, ls_ss, ls_rs,
+    loc, y_sems, z_sems, wz_sems, wx_sems, wc_sems, ar_sems, ig_sems, pc_sems, px_sems, pz_sems,
+    ls_sems,
 ):
     grp = lax.axis_index("grp")
     t = lax.axis_index("tp")
@@ -62,11 +89,10 @@
     def tp_of(y_, h_):
         return (grp, y_ * 2 + h_)
 
-    def remote(src, dst, ss, rs, device):
-        return pltpu.make_async_remote_copy(
-            src_ref=src, dst_ref=dst, send_sem=ss, recv_sem=rs, device_id=device,
-            device_id_type=MESH,
-        )
+    sent = []
+
+    def remote(src, dst, sems, at, device):
+        return Copy(sent, src, dst, sems, at, device)
 
     locals_ = [
         pltpu.make_async_copy(w_snap, w_s.at[grp], loc.at[0]),
@@ -86,8 +112,8 @@
     for d in (1, 2, 3):
         peers.append(grp_of(lo, (x + d) % 4, core))
         peers.append(grp_of((lo + d) % 4, x, core))
-    for j in range(1, 8):
-        peers.append(tp_of((y + j // 2) % 4, (hi + j % 2) % 2))
+        peers.append(tp_of((y + d) % 4, hi))
+    peers.append(tp_of(y, 1 - hi))
     for peer in peers:
         pl.semaphore_signal(barrier, inc=1, device_id=peer, device_id_type=MESH)
     vec[...] = jnp.zeros_like(vec)
@@ -100,7 +126,7 @@
         row = y if i < 4 else (y - STEP[i] + 4) % 4
         ref = buf.at[row * 2 + half_of, pl.ds(HALF[i] * size, size)]
         return remote(
-            ref, ref, y_ss.at[k, i], y_rs.at[k, i], tp_of((y + STEP[i] + 4) % 4, hi)
+            ref, ref, y_sems, (k, i), tp_of((y + STEP[i] + 4) % 4, hi)
         )
 
     def y_arrival(k, i):
@@ -108,31 +134,64 @@
         half_of = hi if k < 2 else 1 - hi
         row = (y - STEP[i] * (1 if i < 4 else 2) + 4) % 4
         ref = buf.at[row * 2 + half_of, pl.ds(HALF[i] * size, size)]
-        return remote(ref, ref, y_ss.at[k, i], y_rs.at[k, i], tp_of(y, hi))
+        return remote(ref, ref, y_sems, (k, i), tp_of(y, hi))
 
     def far_copy(k, half, slot):
         buf, size = ((a_s, 256), (a_e, 192))[k]
         ref = buf.at[slot, pl.ds(half * size, size)]
-        return remote(ref, ref, z_ss.at[k, half], z_rs.at[k, half], tp_of(y, 1 - hi))
+        return remote(ref, ref, z_sems, (k, half), tp_of(y, 1 - hi))
 
     weights = (w_s, w_o)
 
-    def wz_copy(m, d, source):
+    def wz_copy(m, way, step, source):
         ref = weights[m].at[source * 8 + x * 2 + core]
         return remote(
-            ref, ref, wz_ss.at[m, d], wz_rs.at[m, d], grp_of((lo + d) % 4, x, core)
-        )
+            ref, ref, wz_sems, (m, way, step),
+            grp_of((lo + (1, 3)[way]) % 4, x, core),
+        )
+
+    def wz_first(m):
+        wz_copy(m, 0, 0, lo).start(lo < 3)
+        wz_copy(m, 1, 0, lo).start(lo > 0)
+
+    def wz_step(m, step):
+        for way in (0, 1):
+            source = (lo + (step + 1) * (-1, 1)[way] + 4) % 4
+            came = (lo > step, lo < 3 - step)[way]
+            wz_copy(m, way, step, source).wait_recv(came)
+            if step < 2:
+                wz_copy(m, way, step + 1, source).start(came & (lo < 3, lo > 0)[way])
+            for d in (2, 1, 3):
+                wx_copy(m, 1 + 3 * way + step, d, x).start(came)
+            wc_copy(m, 1 + 3 * way + step, 0, core).start(came)
+
+    def line(b):
+        if b == 0:
+            return lo, None
+        step = (b - 1) % 3
+        way = (b - 1) // 3
+        return (lo + (step + 1) * (-1, 1)[way] + 4) % 4, (lo > step, lo < 3 - step)[way]
+
+    def w_pass(m, b):
+        for d in (1, 3, 2):
+            wx_copy(m, b, d, (x - d + 4) % 4).wait_recv(line(b)[1])
+            wc_copy(m, b, d, core).start(line(b)[1])
+
+    def w_done(m):
+        for b in range(7):
+            for d in range(4):
+                wc_copy(m, b, d, 1 - core).wait_recv(line(b)[1])
 
     def wx_copy(m, b, d, x_):
-        ref = weights[m].at[((lo - b + 4) % 4) * 8 + x_ * 2 + core]
-        return remote(
-            ref, ref, wx_ss.at[m, b, d], wx_rs.at[m, b, d], grp_of(lo, (x + d) % 4, core)
+        ref = weights[m].at[line(b)[0] * 8 + x_ * 2 + core]
+        return remote(
+            ref, ref, wx_sems, (m, b, d), grp_of(lo, (x + d) % 4, core)
         )
 
     def wc_copy(m, b, d, c_):
-        ref = weights[m].at[((lo - b + 4) % 4) * 8 + ((x - d + 4) % 4) * 2 + c_]
-        return remote(
-            ref, ref, wc_ss.at[m, b, d], wc_rs.at[m, b, d], grp_of(lo, x, 1 - core)
+        ref = weights[m].at[line(b)[0] * 8 + ((x - d + 4) % 4) * 2 + c_]
+        return remote(
+            ref, ref, wc_sems, (m, b, d), grp_of(lo, x, 1 - core)
         )
 
     def w_spread(m, b):
@@ -143,7 +202,7 @@
     def ar_copy(which, buf, j, slot):
         ref = buf.at[slot]
         return remote(
-            ref, ref, ar_ss.at[which, j], ar_rs.at[which, j],
+            ref, ref, ar_sems, (which, j),
             tp_of((y + j // 2) % 4, (hi + j % 2) % 2),
         )
 
@@ -166,7 +225,7 @@
             ref, device = ig.at[lo, pl.ds(x_ * 2, 2)], grp_of(lo, (x + i) % 4, core)
         else:
             ref, device = ig.at[l_], grp_of((lo + i - 3) % 4, x, core)
-        return remote(ref, ref, ig_ss.at[i], ig_rs.at[i], device)
+        return remote(ref, ref, ig_sems, (i,), device)
 
     def multiply(h_ref, buf, w_ref, half_of):
         def body(i, carry):
@@ -180,89 +239,87 @@
     def turn(half_of):
         def body(i, carry):
             k = ((y + i) % 4) * 2 + half_of
-            a_t[pl.ds(k * 512, 512), :] = a_e[k].T
+            turned = a_e[k].T
+            for b in range(4):
+                at = (half_of * 2 + b // 2) * 8 + (b % 2) * 4 + (y + i) % 4
+                a_t[at] = turned[b * 128 : b * 128 + 128, :]
             return carry
 
         lax.fori_loop(0, 4, body, 0)
+
+    def y_pass(k):
+        for i in (0, 2):
+            y_arrival(k, i).wait_recv()
+            y_copy(k, 4 + i // 2).start()
+
+    def y_rest(k):
+        for i in (1, 3, 4, 5):
+            y_arrival(k, i).wait_recv()
 
     for i in (0, 1):
         locals_[i].wait()
-    for d in (2, 1, 3):
-        wz_copy(0, d, lo).start()
-    w_spread(0, 0)
-    for i in range(4):
+    wz_first(0)
+    for i in (0, 2, 1, 3):
         y_copy(0, i).start()
     for half in (0, 1):
         far_copy(0, half, t).start()
+    w_spread(0, 0)
     for i in (2, 3, 4):
         locals_[i].wait()
-    for d in (2, 1, 3):
-        wz_copy(1, d, lo).start()
+    for i in (0, 2, 1, 3):
+        y_copy(1, i).start()
     w_spread(1, 0)
-    for i in range(4):
-        y_copy(1, i).start()
-    for half in (0, 1):
-        far_copy(1, half, t).start()
+    wz_step(0, 0)
     for i in (5, 6, 7):
         locals_[i].wait()
     h_s[...] = r_s[...].astype(F32)
     h_e[...] = r_e[...].astype(F32)
-
-    for b in (1, 3, 2):
-        wz_copy(0, b, (lo - b + 4) % 4).wait_recv()
-        w_spread(0, b)
-    for i in (0, 2):
-        y_arrival(0, i).wait_recv()
-        y_copy(0, 4 + i // 2).start()
-    for b in (1, 3, 2):
-        wz_copy(1, b, (lo - b + 4) % 4).wait_recv()
-        w_spread(1, b)
-    for i in (0, 2):
-        y_arrival(1, i).wait_recv()
-        y_copy(1, 4 + i // 2).start()
-    for half in (0, 1):
-        far_copy(0, half, t_far).wait_recv()
-    for i in range(4):
+    wz_step(0, 1)
+    y_pass(0)
+    wz_step(0, 2)
+    y_pass(1)
+    w_pass(0, 0)
+    far_copy(0, 0, t_far).wait_recv()
+    for i in (0, 3):
         y_copy(2, i).start()
-    for b in (0, 1, 3, 2):
-        for d in (1, 3, 2):
-            wx_copy(0, b, d, (x - d + 4) % 4).wait_recv()
-            wc_copy(0, b, d, core).start()
-    for i in (0, 2):
-        y_arrival(2, i).wait_recv()
-        y_copy(2, 4 + i // 2).start()
-    for b in range(4):
-        for d in range(4):
-            wc_copy(0, b, d, 1 - core).wait_recv()
-    for i in (1, 3, 4, 5):
-        y_arrival(0, i).wait_recv()
+    far_copy(1, 0, t).start()
+    wz_first(1)
+    for b in (1, 4):
+        w_pass(0, b)
+    far_copy(0, 1, t_far).wait_recv()
+    for i in (2, 1):
+        y_copy(2, i).start()
+    far_copy(1, 1, t).start()
+    wz_step(1, 0)
+    for b in (2, 5, 3, 6):
+        w_pass(0, b)
+    w_pass(1, 0)
+    wz_step(1, 1)
+    y_pass(2)
+    w_done(0)
+    wz_step(1, 2)
+    y_rest(0)
     multiply(h_s, a_s, w_s, hi)
-    for half in (0, 1):
-        far_copy(1, half, t_far).wait_recv()
-    for i in range(4):
+    for b in (1, 4):
+        w_pass(1, b)
+    y_rest(1)
+    far_copy(1, 0, t_far).wait_recv()
+    for i in (0, 3):
         y_copy(3, i).start()
-    for i in (1, 3, 4, 5):
-        y_arrival(1, i).wait_recv()
-    turn(hi)
-    for b in (0, 1, 3, 2):
-        for d in (1, 3, 2):
-            wx_copy(1, b, d, (x - d + 4) % 4).wait_recv()
-            wc_copy(1, b, d, core).start()
-    for i in (1, 3, 4, 5):
-        y_arrival(2, i).wait_recv()
+    far_copy(1, 1, t_far).wait_recv()
+    for i in (2, 1):
+        y_copy(3, i).start()
+    for b in (2, 5, 3, 6):
+        w_pass(1, b)
+    y_rest(2)
     multiply(h_s, a_s, w_s, 1 - hi)
 
     ar_s[t] = jnp.zeros((8, 128), F32)
     for b in range(4):
         ar_s[t, b : b + 1, :] = square_rows(h_s, b)
     ar_start(0, ar_s)
-    for i in (0, 2):
-        y_arrival(3, i).wait_recv()
-        y_copy(3, 4 + i // 2).start()
-    for b in range(4):
-        for d in range(4):
-            wc_copy(1, b, d, 1 - core).wait_recv()
-    multiply(h_e, a_e, w_o, hi)
+    y_pass(3)
+    turn(hi)
     gain = gain_ref[...].astype(F32)
 
     factor_s = lax.rsqrt(ar_finish(0, ar_s) / WIDTH + EPS)
@@ -281,6 +338,8 @@
         square = jnp.sum(total * total, axis=1, keepdims=True)
         ar_p[t, s : s + 1, :] = jnp.broadcast_to(square, (1, 128))
     ar_start(1, ar_p)
+    w_done(1)
+    multiply(h_e, a_e, w_o, hi)
     norm_s = lax.rsqrt(ar_finish(1, ar_p) / WIDTH + EPS)
     for s in range(2):
         row = (pool_s[s : s + 1, :] * lanes4(norm_s[s : s + 1, :])).astype(BF16).astype(F32)
@@ -293,8 +352,7 @@
     for i in (2, 1, 3):
         ig_copy(i, lo, x, core).start()
 
-    for i in (1, 3, 4, 5):
-        y_arrival(3, i).wait_recv()
+    y_rest(3)
     multiply(h_e, a_e, w_o, 1 - hi)
     ar_e[t] = jnp.zeros((8, 128), F32)
     for b in range(3):
@@ -371,7 +429,7 @@
 
     l_c[core] = jnp.broadcast_to(loss, (8, 128))
     pair_loss = remote(
-        l_c.at[core], l_c.at[core], ls_ss.at[0], ls_rs.at[0], grp_of(lo, x, 1 - core)
+        l_c.at[core], l_c.at[core], ls_sems, (0,), grp_of(lo, x, 1 - core)
     )
     pair_loss.start()
 
@@ -403,74 +461,83 @@
 
     def pc_copy(i, x_):
         return remote(
-            psend.at[x_], precv.at[x_], pc_ss.at[i], pc_rs.at[i], grp_of(lo, x, 1 - core)
-        )
-
-    def px_copy(i, d, dst):
-        return remote(
-            xsend.at[i, d], xrecv.at[i, d], px_ss.at[i, d], px_rs.at[i, d], grp_of(lo, dst, core)
+            psend.at[x_], precv.at[x_], pc_sems, (i,), grp_of(lo, x, 1 - core)
+        )
+
+    up = {2: 1, 1: 1, 3: -1, 0: -1}
+
+    def px_copy(stage, side, d):
+        at = stage + side
+        return remote(
+            xsend.at[at, d], xrecv.at[at, d], px_sems, (at, d),
+            grp_of(lo, (x + (up[d], 1, -1)[at] + 4) % 4, core),
         )
 
     def pz_copy(d):
         return remote(
-            zsend.at[d], zrecv.at[d], pz_ss.at[d], pz_rs.at[d], grp_of((lo + d) % 4, x, core)
+            zsend.at[d], zrecv.at[d], pz_sems, (d,), grp_of((lo + d) % 4, x, core)
         )
 
     turns = (2, 1, 3, 0)
     for i in range(4):
         x_ = (x + turns[i]) % 4
-
-        def other(l_, carry, x_=x_):
-            at = pl.ds((l_ * 8 + x_ * 2 + 1 - core) * 128, 128)
-            psend[x_, l_] = jnp.dot(
-                a_t[at, :], dh[...], preferred_element_type=F32
-            ).astype(BF16)
-            return carry
-
-        def mine(l_, carry, x_=x_):
-            at = pl.ds((l_ * 8 + x_ * 2 + core) * 128, 128)
-            own[x_, l_] = jnp.dot(a_t[at, :], dh[...], preferred_element_type=F32)
-            return carry
-
-        lax.fori_loop(0, 4, other, 0)
+        at = pl.ds((x_ * 2 + 1 - core) * 4, 4)
+        part = jnp.dot(a_t[at].reshape(512, ETOK), dh[...], preferred_element_type=F32)
+        psend[x_] = part.astype(BF16).reshape(4, 128, COLS)
         pc_copy(i, x_).start()
-        lax.fori_loop(0, 4, mine, 0)
+        at = pl.ds((x_ * 2 + core) * 4, 4)
+        part = jnp.dot(a_t[at].reshape(512, ETOK), dh[...], preferred_element_type=F32)
+        own[x_] = part.reshape(4, 128, COLS)
 
     pair_loss.wait_recv()
     l_x[x] = l_c[0] + l_c[1]
 
     def lx_copy(d, slot):
         return remote(
-            l_x.at[slot], l_x.at[slot], ls_ss.at[d], ls_rs.at[d], grp_of(lo, (x + d) % 4, core)
+            l_x.at[slot], l_x.at[slot], ls_sems, (d,), grp_of(lo, (x + d) % 4, core)
         )
 
     def lz_copy(d, slot):
         return remote(
-            l_z.at[slot], l_z.at[slot], ls_ss.at[3 + d], ls_rs.at[3 + d],
+            l_z.at[slot], l_z.at[slot], ls_sems, (3 + d,),
             grp_of((lo + d) % 4, x, core),
         )
 
     for d in (1, 2, 3):
         lx_copy(d, x).start()
-    for i in range(3):
-        x_ = (x + turns[i]) % 4
-        pc_copy(i, x_).wait_recv()
-        for d in (2, 1, 3, 0):
-            l_ = (lo + d) % 4
-            xsend[i, d] = (own[x_, l_] + precv[x_, l_].astype(F32)).astype(BF16)
-            px_copy(i, d, x_).start()
-    pc_copy(3, x).wait_recv()
+    def pair_sum(x_, d):
+        l_ = (lo + d) % 4
+        return own[x_, l_] + precv[x_, l_].astype(F32)
+
+    pc_copy(0, x).wait_recv()
+    for d in (2, 3, 1, 0):
+        xsend[0, d] = pair_sum((x + 2) % 4, d).astype(BF16)
+        px_copy(0, 0, d).start()
+    pc_copy(1, x).wait_recv()
+    for d in (3, 0):
+        xsend[1, d] = pair_sum((x + 1) % 4, d).astype(BF16)
+        px_copy(1, 0, d).start()
+    pc_copy(2, x).wait_recv()
+    for d in (2, 1):
+        xsend[2, d] = pair_sum((x + 3) % 4, d).astype(BF16)
+        px_copy(1, 1, d).start()
     for d in (1, 2, 3):
         lx_copy(d, (x - d + 4) % 4).wait_recv()
     l_z[lo] = (l_x[0] + l_x[1]) + (l_x[2] + l_x[3])
     for d in (1, 2, 3):
         lz_copy(d, lo).start()
-    for d in (2, 1, 3, 0):
-        l_ = (lo + d) % 4
-        total = own[x, l_] + precv[x, l_].astype(F32)
-        for i in (1, 2, 0):
-            px_copy(i, d, x).wait_recv()
-        total = total + (xrecv[0, d].astype(F32) + xrecv[1, d].astype(F32) + xrecv[2, d].astype(F32))
+    for d in (2, 3, 1, 0):
+        side = 0 if up[d] == 1 else 1
+        px_copy(0, 0, d).wait_recv()
+        total = pair_sum((x + up[d] + 4) % 4, d) + xrecv[0, d].astype(F32)
+        xsend[1 + side, d] = total.astype(BF16)
+        px_copy(1, side, d).start()
+    pc_copy(3, x).wait_recv()
+    for d in (2, 3, 1, 0):
+        total = pair_sum(x, d)
+        for side in (0, 1):
+            px_copy(1, side, d).wait_recv()
+        total = total + (xrecv[1, d].astype(F32) + xrecv[2, d].astype(F32))
         if d == 0:
             grad_ref[...] = total
         else:
@@ -483,34 +550,8 @@
         pz_copy(d).wait_recv()
     grad_ref[...] += (zrecv[1].astype(F32) + zrecv[2].astype(F32)) + zrecv[3].astype(F32)
 
-    for k in range(4):
-        for i in range(6):
-            y_copy(k, i).wait_send()
-    for k in range(2):
-        for half in (0, 1):
-            far_copy(k, half, t).wait_send()
-        for d in (1, 2, 3):
-            wz_copy(k, d, lo).wait_send()
-        for b in range(4):
-            for d in (1, 2, 3):
-                wx_copy(k, b, d, x).wait_send()
-            for d in range(4):
-                wc_copy(k, b, d, core).wait_send()
-    for which, buf in enumerate((ar_s, ar_p, ar_e, ar_g)):
-        for j in range(1, 8):
-            ar_copy(which, buf, j, t).wait_send()
-    for i in range(7):
-        ig_copy(i, lo, x, core).wait_send()
-    pair_loss.wait_send()
-    for d in (1, 2, 3):
-        lx_copy(d, x).wait_send()
-        lz_copy(d, lo).wait_send()
-        pz_copy(d).wait_send()
-    for i in range(4):
-        pc_copy(i, x).wait_send()
-    for i in range(3):
-        for d in range(4):
-            px_copy(i, d, x).wait_send()
+    for copy in sent:
+        copy.wait_send()
 
 
 def shards(
@@ -521,6 +562,10 @@
     vmem = pl.BlockSpec(memory_space=pltpu.VMEM)
     smem = pl.BlockSpec(memory_space=pltpu.SMEM)
     dma = pltpu.SemaphoreType.DMA
+
+    def both(shape):
+        return (dma(shape), dma(shape))
+
     loss, grad, index = pl.pallas_call(
         kernel,
         out_shape=(
@@ -539,7 +584,7 @@
             pltpu.VMEM((ETOK, COLS), BF16),
             pltpu.VMEM((STOK, COLS), F32),
             pltpu.VMEM((ETOK, COLS), F32),
-            pltpu.VMEM((WIDTH, ETOK), BF16),
+            pltpu.VMEM((32, 128, ETOK), BF16),
             pltpu.VMEM((8, 8, 128), F32),
             pltpu.VMEM((8, 8, 128), F32),
             pltpu.VMEM((8, 8, 128), F32),
@@ -565,17 +610,17 @@
             pltpu.VMEM((4, 8, 128), F32),
             pltpu.VMEM((4, 8, 128), F32),
             dma((8,)),
-            dma((4, 6)), dma((4, 6)),
-            dma((2, 2)), dma((2, 2)),
-            dma((2, 4)), dma((2, 4)),
-            dma((2, 4, 4)), dma((2, 4, 4)),
-            dma((2, 4, 4)), dma((2, 4, 4)),
-            dma((4, 8)), dma((4, 8)),
-            dma((7,)), dma((7,)),
-            dma((4,)), dma((4,)),
-            dma((3, 4)), dma((3, 4)),
-            dma((4,)), dma((4,)),
-            dma((7,)), dma((7,)),
+            both((4, 6)),
+            both((2, 2)),
+            both((2, 2, 3)),
+            both((2, 7, 4)),
+            both((2, 7, 4)),
+            both((4, 8)),
+            both((7,)),
+            both((4,)),
+            both((3, 4)),
+            both((4,)),
+            both((7,)),
         ],
         compiler_params=pltpu.CompilerParams(
             collective_id=0, has_side_effects=True, vmem_limit_bytes=56 * 2**20

time: 176 us -> 149 us (0.85)
  Pallas kernels: 169 us -> 143 us
    pallas_call x1, Pallas kernels: 169 us -> 143 us  [shards(): pl.pallas_call(kernel, out_shape=(jax.ShapeDtypeStruct((1, 1), F32), jax....]
where the time goes in v2:
time: 149 us
  Pallas kernels  143 us (96%)
  local copies, waits for them, and re-layouts  3.51 us (2%)
  between operations  2.47 us (2%)
    pallas_call x1, Pallas kernels, shards(): pl.pallas_call(kernel, out_shape=(jax.ShapeDtypeStruct((1, 1), F32), jax....  143 us

profile of v2, /device:TPU:2, one launch (start us, length us, event | category | flops | bytes accessed | tf_op | source)
XLA Modules:
  0.0 148.9 jit_solution(1074783732301567467)
XLA Ops:
  0.6 0.0 copy-start.1
  0.6 0.7 copy-done.1
  1.3 0.6 reshape.31.gain_ref
  1.9 143.0 %shard_map.139 = (f32[1,1]{1,0:T(1,128)}, f32[128,512]{1,0:T(8,128)}, bf16[2,512]{1,0:T(2,128)(2,1)}) custom-call(bf16[128,512]{1,0:T(8,128)(2,1)} %bitcast.11, bf16[128,512]{1,0:T(8,128)(2,1)} %bitcast.12, bf16[256,512]{1,0:T(8,128)(2,1)} %bitcast.9, bf16[256,512]{1,0:T(8,128)(2,1)} %bitcast.10, bf16[128,512]{1,0:T(8,128)(2,1)} %w_out.1, ...), custom_call_target="tpu_custom_call" | custom-call | tf_op jit(solution)/shard_map/pallas_call | solution.py:569
  145.6 0.0 copy-start
  145.6 1.7 %copy.19 = f32[128,512]{1,0:T(8,128)} copy(f32[128,512]{1,0:T(8,128)} %get-tuple-element.13) | data formatting | bytes 524288
  147.2 0.0 copy-done
  147.2 0.6 copy.20
Async XLA Ops:
  0.6 0.7 copy-start.1
  145.6 1.7 %copy-start = (bf16[2,512]{1,0:T(2,128)(2,1)S(1)}, bf16[2,512]{1,0:T(2,128)(2,1)}, u32[]{:S(2)}) copy-start(bf16[2,512]{1,0:T(2,128)(2,1)} %get-tuple-element.14) | copy-start | bytes 6148

commit v3 on v2

--- a/solution.py
+++ b/solution.py
@@ -18,8 +18,7 @@
 HI = lax.Precision.HIGHEST
 F32 = jnp.float32
 BF16 = jnp.bfloat16
-HALF = (0, 1, 1, 0, 0, 1)
-STEP = (1, 1, -1, -1, 1, -1)
+PARTS = 7
 
 
 class Copy:
@@ -120,26 +119,49 @@
     s_full[...] = jnp.zeros_like(s_full)
     pl.semaphore_wait(barrier, len(peers))
 
-    def y_copy(k, i):
-        buf, size = ((a_s, 256), (a_e, 192))[k % 2]
-        half_of = hi if k < 2 else 1 - hi
-        row = y if i < 4 else (y - STEP[i] + 4) % 4
-        ref = buf.at[row * 2 + half_of, pl.ds(HALF[i] * size, size)]
-        return remote(
-            ref, ref, y_sems, (k, i), tp_of((y + STEP[i] + 4) % 4, hi)
-        )
-
-    def y_arrival(k, i):
-        buf, size = ((a_s, 256), (a_e, 192))[k % 2]
-        half_of = hi if k < 2 else 1 - hi
-        row = (y - STEP[i] * (1 if i < 4 else 2) + 4) % 4
-        ref = buf.at[row * 2 + half_of, pl.ds(HALF[i] * size, size)]
-        return remote(ref, ref, y_sems, (k, i), tp_of(y, hi))
-
-    def far_copy(k, half, slot):
-        buf, size = ((a_s, 256), (a_e, 192))[k]
-        ref = buf.at[slot, pl.ds(half * size, size)]
-        return remote(ref, ref, z_sems, (k, half), tp_of(y, 1 - hi))
+    def token_part(part, slot):
+        if part < 4:
+            return a_s.at[slot, pl.ds(part * 128, 128)]
+        return a_e.at[slot, pl.ds((part - 4) * 128, 128)]
+
+    def pass_step(far, part):
+        return 1 if (part + far) % 2 == 0 else -1
+
+    def y_copy(far, part, way):
+        step = (1, -1, pass_step(far, part))[way]
+        row = y if way < 2 else (y - step + 4) % 4
+        ref = token_part(part, row * 2 + (hi if far == 0 else 1 - hi))
+        return remote(ref, ref, y_sems, (far, part, way), tp_of((y + step + 4) % 4, hi))
+
+    def y_arrival(far, part, way):
+        step = (1, -1, 2 * pass_step(far, part))[way]
+        ref = token_part(part, ((y - step + 4) % 4) * 2 + (hi if far == 0 else 1 - hi))
+        return remote(ref, ref, y_sems, (far, part, way), tp_of(y, hi))
+
+    def y_send(far, part):
+        first = 0 if pass_step(far, part) == 1 else 1
+        y_copy(far, part, first).start()
+        y_copy(far, part, 1 - first).start()
+
+    def y_pass(far, part):
+        way = 0 if pass_step(far, part) == 1 else 1
+        y_arrival(far, part, way).wait_recv()
+        y_copy(far, part, 2).start()
+
+    def y_rest(far, parts):
+        for part in parts:
+            y_arrival(far, part, 1 if pass_step(far, part) == 1 else 0).wait_recv()
+            y_arrival(far, part, 2).wait_recv()
+
+    def far_copy(part, slot):
+        ref = token_part(part, slot)
+        return remote(ref, ref, z_sems, (part,), tp_of(y, 1 - hi))
+
+    def far_pass(part):
+        far_copy(part, t_far).wait_recv()
+        if part + 3 < PARTS:
+            far_copy(part + 3, t).start()
+        y_send(1, part)
 
     weights = (w_s, w_o)
 
@@ -247,79 +269,72 @@
 
         lax.fori_loop(0, 4, body, 0)
 
-    def y_pass(k):
-        for i in (0, 2):
-            y_arrival(k, i).wait_recv()
-            y_copy(k, 4 + i // 2).start()
-
-    def y_rest(k):
-        for i in (1, 3, 4, 5):
-            y_arrival(k, i).wait_recv()
-
     for i in (0, 1):
         locals_[i].wait()
     wz_first(0)
-    for i in (0, 2, 1, 3):
-        y_copy(0, i).start()
-    for half in (0, 1):
-        far_copy(0, half, t).start()
+    for part in range(4):
+        y_send(0, part)
+        if part < 3:
+            far_copy(part, t).start()
     w_spread(0, 0)
     for i in (2, 3, 4):
         locals_[i].wait()
-    for i in (0, 2, 1, 3):
-        y_copy(1, i).start()
+    for part in (4, 5, 6):
+        y_send(0, part)
     w_spread(1, 0)
     wz_step(0, 0)
     for i in (5, 6, 7):
         locals_[i].wait()
     h_s[...] = r_s[...].astype(F32)
     h_e[...] = r_e[...].astype(F32)
+    y_pass(0, 0)
+    y_pass(0, 1)
     wz_step(0, 1)
-    y_pass(0)
+    far_pass(0)
+    y_pass(0, 2)
+    y_pass(0, 3)
+    far_pass(1)
     wz_step(0, 2)
-    y_pass(1)
-    w_pass(0, 0)
-    far_copy(0, 0, t_far).wait_recv()
-    for i in (0, 3):
-        y_copy(2, i).start()
-    far_copy(1, 0, t).start()
     wz_first(1)
-    for b in (1, 4):
+    for b in (0, 1, 4):
         w_pass(0, b)
-    far_copy(0, 1, t_far).wait_recv()
-    for i in (2, 1):
-        y_copy(2, i).start()
-    far_copy(1, 1, t).start()
-    wz_step(1, 0)
-    for b in (2, 5, 3, 6):
+    far_pass(2)
+    for part in (4, 5, 6):
+        y_pass(0, part)
+    for b in (2, 5):
+        w_pass(0, b)
+    far_pass(3)
+    for b in (3, 6):
         w_pass(0, b)
     w_pass(1, 0)
+    y_pass(1, 0)
+    y_pass(1, 1)
+    far_pass(4)
+    wz_step(1, 0)
+    w_done(0)
+    y_rest(0, range(4))
+    multiply(h_s, a_s, w_s, hi)
+    y_pass(1, 2)
+    y_pass(1, 3)
+    far_pass(5)
     wz_step(1, 1)
-    y_pass(2)
-    w_done(0)
-    wz_step(1, 2)
-    y_rest(0)
-    multiply(h_s, a_s, w_s, hi)
     for b in (1, 4):
         w_pass(1, b)
-    y_rest(1)
-    far_copy(1, 0, t_far).wait_recv()
-    for i in (0, 3):
-        y_copy(3, i).start()
-    far_copy(1, 1, t_far).wait_recv()
-    for i in (2, 1):
-        y_copy(3, i).start()
-    for b in (2, 5, 3, 6):
-        w_pass(1, b)
-    y_rest(2)
+    y_rest(1, range(4))
     multiply(h_s, a_s, w_s, 1 - hi)
 
     ar_s[t] = jnp.zeros((8, 128), F32)
     for b in range(4):
         ar_s[t, b : b + 1, :] = square_rows(h_s, b)
     ar_start(0, ar_s)
-    y_pass(3)
+    y_pass(1, 4)
+    far_pass(6)
+    wz_step(1, 2)
+    y_pass(1, 5)
+    y_rest(0, (4, 5, 6))
     turn(hi)
+    for b in (2, 5):
+        w_pass(1, b)
     gain = gain_ref[...].astype(F32)
 
     factor_s = lax.rsqrt(ar_finish(0, ar_s) / WIDTH + EPS)
@@ -338,6 +353,9 @@
         square = jnp.sum(total * total, axis=1, keepdims=True)
         ar_p[t, s : s + 1, :] = jnp.broadcast_to(square, (1, 128))
     ar_start(1, ar_p)
+    y_pass(1, 6)
+    for b in (3, 6):
+        w_pass(1, b)
     w_done(1)
     multiply(h_e, a_e, w_o, hi)
     norm_s = lax.rsqrt(ar_finish(1, ar_p) / WIDTH + EPS)
@@ -352,7 +370,7 @@
     for i in (2, 1, 3):
         ig_copy(i, lo, x, core).start()
 
-    y_rest(3)
+    y_rest(1, (4, 5, 6))
     multiply(h_e, a_e, w_o, 1 - hi)
     ar_e[t] = jnp.zeros((8, 128), F32)
     for b in range(3):
@@ -479,59 +497,80 @@
         )
 
     turns = (2, 1, 3, 0)
-    for i in range(4):
+
+    def part_of(x_, c_):
+        rows = a_t[pl.ds((x_ * 2 + c_) * 4, 4)].reshape(512, ETOK)
+        part = jnp.dot(rows, dh[...], preferred_element_type=F32)
+        return part.reshape(4, 128, COLS)
+
+    def give(i):
         x_ = (x + turns[i]) % 4
-        at = pl.ds((x_ * 2 + 1 - core) * 4, 4)
-        part = jnp.dot(a_t[at].reshape(512, ETOK), dh[...], preferred_element_type=F32)
-        psend[x_] = part.astype(BF16).reshape(4, 128, COLS)
+        psend[x_] = part_of(x_, 1 - core).astype(BF16)
         pc_copy(i, x_).start()
-        at = pl.ds((x_ * 2 + core) * 4, 4)
-        part = jnp.dot(a_t[at].reshape(512, ETOK), dh[...], preferred_element_type=F32)
-        own[x_] = part.reshape(4, 128, COLS)
-
-    pair_loss.wait_recv()
-    l_x[x] = l_c[0] + l_c[1]
-
-    def lx_copy(d, slot):
-        return remote(
-            l_x.at[slot], l_x.at[slot], ls_sems, (d,), grp_of(lo, (x + d) % 4, core)
-        )
-
-    def lz_copy(d, slot):
-        return remote(
-            l_z.at[slot], l_z.at[slot], ls_sems, (3 + d,),
-            grp_of((lo + d) % 4, x, core),
-        )
-
-    for d in (1, 2, 3):
-        lx_copy(d, x).start()
+
+    def keep(i):
+        x_ = (x + turns[i]) % 4
+        own[x_] = part_of(x_, core)
+
     def pair_sum(x_, d):
         l_ = (lo + d) % 4
         return own[x_, l_] + precv[x_, l_].astype(F32)
 
+    def direct(d):
+        side = 0 if up[d] == -1 else 1
+        xsend[1 + side, d] = pair_sum((x + (1, 3)[side]) % 4, d).astype(BF16)
+        px_copy(1, side, d).start()
+
+    def relay(d):
+        side = 0 if up[d] == 1 else 1
+        px_copy(0, 0, d).wait_recv()
+        total = pair_sum((x + (1, 3)[side]) % 4, d) + xrecv[0, d].astype(F32)
+        xsend[1 + side, d] = total.astype(BF16)
+        px_copy(1, side, d).start()
+
+    give(0)
+    keep(0)
+    give(1)
+    pair_loss.wait_recv()
+    l_x[x] = l_c[0] + l_c[1]
+
+    def lx_copy(d, slot):
+        return remote(
+            l_x.at[slot], l_x.at[slot], ls_sems, (d,), grp_of(lo, (x + d) % 4, core)
+        )
+
+    def lz_copy(d, slot):
+        return remote(
+            l_z.at[slot], l_z.at[slot], ls_sems, (3 + d,),
+            grp_of((lo + d) % 4, x, core),
+        )
+
+    for d in (1, 2, 3):
+        lx_copy(d, x).start()
     pc_copy(0, x).wait_recv()
     for d in (2, 3, 1, 0):
         xsend[0, d] = pair_sum((x + 2) % 4, d).astype(BF16)
         px_copy(0, 0, d).start()
+    keep(1)
+    give(2)
+    keep(2)
+    give(3)
     pc_copy(1, x).wait_recv()
-    for d in (3, 0):
-        xsend[1, d] = pair_sum((x + 1) % 4, d).astype(BF16)
-        px_copy(1, 0, d).start()
     pc_copy(2, x).wait_recv()
-    for d in (2, 1):
-        xsend[2, d] = pair_sum((x + 3) % 4, d).astype(BF16)
-        px_copy(1, 1, d).start()
+    relay(2)
+    relay(3)
+    direct(3)
+    direct(2)
+    keep(3)
     for d in (1, 2, 3):
         lx_copy(d, (x - d + 4) % 4).wait_recv()
     l_z[lo] = (l_x[0] + l_x[1]) + (l_x[2] + l_x[3])
     for d in (1, 2, 3):
         lz_copy(d, lo).start()
-    for d in (2, 3, 1, 0):
-        side = 0 if up[d] == 1 else 1
-        px_copy(0, 0, d).wait_recv()
-        total = pair_sum((x + up[d] + 4) % 4, d) + xrecv[0, d].astype(F32)
-        xsend[1 + side, d] = total.astype(BF16)
-        px_copy(1, side, d).start()
+    relay(1)
+    direct(1)
+    direct(0)
+    relay(0)
     pc_copy(3, x).wait_recv()
     for d in (2, 3, 1, 0):
         total = pair_sum(x, d)
@@ -610,8 +649,8 @@
             pltpu.VMEM((4, 8, 128), F32),
             pltpu.VMEM((4, 8, 128), F32),
             dma((8,)),
-            both((4, 6)),
-            both((2, 2)),
+            both((2, PARTS, 3)),
+            both((PARTS,)),
             both((2, 2, 3)),
             both((2, 7, 4)),
             both((2, 7, 4)),

time: 149 us -> 137 us (0.919)
  Pallas kernels: 143 us -> 131 us
    pallas_call x1, Pallas kernels: 143 us -> 131 us  [shards(): pl.pallas_call(kernel, out_shape=(jax.ShapeDtypeStruct((1, 1), F32), jax....]
where the time goes in v3:
time: 137 us
  Pallas kernels  131 us (96%)
  local copies, waits for them, and re-layouts  3.51 us (3%)
  between operations  2.47 us (2%)
    pallas_call x1, Pallas kernels, shards(): pl.pallas_call(kernel, out_shape=(jax.ShapeDtypeStruct((1, 1), F32), jax....  131 us
    unnamed x6, local copies, waits for them, and re-layouts  2.93 us

profile of v3, /device:TPU:2, one launch (start us, length us, event | category | flops | bytes accessed | tf_op | source)
XLA Modules:
  0.0 136.5 jit_solution(838538492977693002)
XLA Ops:
  0.6 0.0 copy-start.1
  0.6 0.7 copy-done.1
  1.3 0.6 reshape.31.gain_ref
  1.9 130.6 %shard_map.139 = (f32[1,1]{1,0:T(1,128)}, f32[128,512]{1,0:T(8,128)}, bf16[2,512]{1,0:T(2,128)(2,1)}) custom-call(bf16[128,512]{1,0:T(8,128)(2,1)} %bitcast.11, bf16[128,512]{1,0:T(8,128)(2,1)} %bitcast.12, bf16[256,512]{1,0:T(8,128)(2,1)} %bitcast.9, bf16[256,512]{1,0:T(8,128)(2,1)} %bitcast.10, bf16[128,512]{1,0:T(8,128)(2,1)} %w_out.1, ...), custom_call_target="tpu_custom_call" | custom-call | tf_op jit(solution)/shard_map/pallas_call | solution.py:608
  133.2 0.0 copy-start
  133.2 1.7 %copy.19 = f32[128,512]{1,0:T(8,128)} copy(f32[128,512]{1,0:T(8,128)} %get-tuple-element.13) | data formatting | bytes 524288
  134.8 0.0 copy-done
  134.8 0.6 copy.20
Async XLA Ops:
  0.6 0.7 copy-start.1
  133.2 1.7 %copy-start = (bf16[2,512]{1,0:T(2,128)(2,1)S(1)}, bf16[2,512]{1,0:T(2,128)(2,1)}, u32[]{:S(2)}) copy-start(bf16[2,512]{1,0:T(2,128)(2,1)} %get-tuple-element.14) | copy-start | bytes 6148

commit v4 on v3

--- a/solution.py
+++ b/solution.py
@@ -289,23 +289,25 @@
     h_e[...] = r_e[...].astype(F32)
     y_pass(0, 0)
     y_pass(0, 1)
-    wz_step(0, 1)
     far_pass(0)
     y_pass(0, 2)
     y_pass(0, 3)
+    wz_step(0, 1)
     far_pass(1)
     wz_step(0, 2)
     wz_first(1)
-    for b in (0, 1, 4):
-        w_pass(0, b)
+    w_pass(0, 0)
+    w_pass(0, 1)
+    w_pass(0, 4)
     far_pass(2)
-    for part in (4, 5, 6):
-        y_pass(0, part)
-    for b in (2, 5):
-        w_pass(0, b)
+    y_pass(0, 4)
+    y_pass(0, 5)
+    y_pass(0, 6)
+    w_pass(0, 2)
+    w_pass(0, 5)
     far_pass(3)
-    for b in (3, 6):
-        w_pass(0, b)
+    w_pass(0, 3)
+    w_pass(0, 6)
     w_pass(1, 0)
     y_pass(1, 0)
     y_pass(1, 1)
@@ -415,7 +417,11 @@
     ar_g[t, 12:13, :] = sims[1:2, 256:384]
     ar_g[t, 13:14, :] = sims[3:4, 256:384]
     ar_g[t, 16:24, :] = gram
+    left = list(sent)
+    sent.clear()
     ar_start(3, ar_g)
+    for copy in left:
+        copy.wait_send()
     both = ar_finish(3, ar_g)
 
     gram = both[16:24, :]
@@ -482,7 +488,8 @@
             psend.at[x_], precv.at[x_], pc_sems, (i,), grp_of(lo, x, 1 - core)
         )
 
-    up = {2: 1, 1: 1, 3: -1, 0: -1}
+    up = (1, -1, 1, -1)
+    line_of = (3 * (1 - lo // 2), 2 - lo // 2, lo + 1 - 2 * (lo % 2), lo)
 
     def px_copy(stage, side, d):
         at = stage + side
@@ -491,10 +498,14 @@
             grp_of(lo, (x + (up[d], 1, -1)[at] + 4) % 4, core),
         )
 
-    def pz_copy(d):
-        return remote(
-            zsend.at[d], zrecv.at[d], pz_sems, (d,), grp_of((lo + d) % 4, x, core)
-        )
+    def pz_copy(k):
+        d = (line_of[k] - lo + 4) % 4
+        return remote(
+            zsend.at[k], zrecv.at[d], pz_sems, (d,), grp_of(line_of[k], x, core)
+        )
+
+    def pz_arrival(d):
+        return remote(zsend.at[d], zrecv.at[d], pz_sems, (d,), grp_of(lo, x, core))
 
     turns = (2, 1, 3, 0)
 
@@ -513,7 +524,7 @@
         own[x_] = part_of(x_, core)
 
     def pair_sum(x_, d):
-        l_ = (lo + d) % 4
+        l_ = line_of[d]
         return own[x_, l_] + precv[x_, l_].astype(F32)
 
     def direct(d):
@@ -548,7 +559,7 @@
     for d in (1, 2, 3):
         lx_copy(d, x).start()
     pc_copy(0, x).wait_recv()
-    for d in (2, 3, 1, 0):
+    for d in range(4):
         xsend[0, d] = pair_sum((x + 2) % 4, d).astype(BF16)
         px_copy(0, 0, d).start()
     keep(1)
@@ -557,27 +568,31 @@
     give(3)
     pc_copy(1, x).wait_recv()
     pc_copy(2, x).wait_recv()
-    relay(2)
-    relay(3)
-    direct(3)
-    direct(2)
+    left = list(sent[:8])
+    del sent[:8]
+    for copy in left:
+        copy.wait_send()
+    relay(0)
+    relay(1)
+    direct(1)
+    direct(0)
     keep(3)
     for d in (1, 2, 3):
         lx_copy(d, (x - d + 4) % 4).wait_recv()
     l_z[lo] = (l_x[0] + l_x[1]) + (l_x[2] + l_x[3])
     for d in (1, 2, 3):
         lz_copy(d, lo).start()
-    relay(1)
-    direct(1)
-    direct(0)
-    relay(0)
+    relay(2)
+    direct(2)
+    direct(3)
+    relay(3)
     pc_copy(3, x).wait_recv()
-    for d in (2, 3, 1, 0):
+    for d in range(4):
         total = pair_sum(x, d)
         for side in (0, 1):
             px_copy(1, side, d).wait_recv()
         total = total + (xrecv[1, d].astype(F32) + xrecv[2, d].astype(F32))
-        if d == 0:
+        if d == 3:
             grad_ref[...] = total
         else:
             zsend[d] = total.astype(BF16)
@@ -586,7 +601,7 @@
         lz_copy(d, (lo - d + 4) % 4).wait_recv()
     loss_ref[...] = ((l_z[0] + l_z[1]) + (l_z[2] + l_z[3]))[0:1, 0:1] / 64.0
     for d in (1, 3, 2):
-        pz_copy(d).wait_recv()
+        pz_arrival(d).wait_recv()
     grad_ref[...] += (zrecv[1].astype(F32) + zrecv[2].astype(F32)) + zrecv[3].astype(F32)
 
     for copy in sent:

time: 137 us -> 135 us (0.985); the launches traced: 137 us -> 133 us
  Pallas kernels: 131 us -> 127 us
    pallas_call x1, Pallas kernels: 131 us -> 127 us  [shards(): pl.pallas_call(kernel, out_shape=(jax.ShapeDtypeStruct((1, 1), F32), jax....]
where the time goes in v4:
time: 135 us; the launch traced here: 133 us
  Pallas kernels  127 us (94%)
  local copies, waits for them, and re-layouts  3.51 us (3%)
  between operations  2.47 us (2%)
    pallas_call x1, Pallas kernels, shards(): pl.pallas_call(kernel, out_shape=(jax.ShapeDtypeStruct((1, 1), F32), jax....  127 us
    unnamed x6, local copies, waits for them, and re-layouts  2.93 us

profile of v4, /device:TPU:2, one launch (start us, length us, event | category | flops | bytes accessed | tf_op | source)
XLA Modules:
  0.0 132.9 jit_solution(12349569286644027508)
XLA Ops:
  0.6 0.0 copy-start.1
  0.6 0.7 copy-done.1
  1.3 0.6 reshape.31.gain_ref
  1.9 126.9 %shard_map.139 = (f32[1,1]{1,0:T(1,128)}, f32[128,512]{1,0:T(8,128)}, bf16[2,512]{1,0:T(2,128)(2,1)}) custom-call(bf16[128,512]{1,0:T(8,128)(2,1)} %bitcast.11, bf16[128,512]{1,0:T(8,128)(2,1)} %bitcast.12, bf16[256,512]{1,0:T(8,128)(2,1)} %bitcast.9, bf16[256,512]{1,0:T(8,128)(2,1)} %bitcast.10, bf16[128,512]{1,0:T(8,128)(2,1)} %w_out.1, ...), custom_call_target="tpu_custom_call" | custom-call | tf_op jit(solution)/shard_map/pallas_call | solution.py:623
  129.5 0.0 copy-start
  129.5 1.7 %copy.19 = f32[128,512]{1,0:T(8,128)} copy(f32[128,512]{1,0:T(8,128)} %get-tuple-element.13) | data formatting | bytes 524288
  131.2 0.0 copy-done
  131.2 0.6 copy.20
Async XLA Ops:
  0.6 0.7 copy-start.1
  129.5 1.7 %copy-start = (bf16[2,512]{1,0:T(2,128)(2,1)S(1)}, bf16[2,512]{1,0:T(2,128)(2,1)}, u32[]{:S(2)}) copy-start(bf16[2,512]{1,0:T(2,128)(2,1)} %get-tuple-element.14) | copy-start | bytes 6148

commit v5 on v4

--- a/solution.py
+++ b/solution.py
@@ -337,7 +337,7 @@
     turn(hi)
     for b in (2, 5):
         w_pass(1, b)
-    gain = gain_ref[...].astype(F32)
+    gain = gain_ref[...].astype(F32).reshape(1, COLS)
 
     factor_s = lax.rsqrt(ar_finish(0, ar_s) / WIDTH + EPS)
     ar_p[t] = jnp.zeros((8, 128), F32)
@@ -384,13 +384,6 @@
         ig_copy(i, lo, x, core).start()
     turn(1 - hi)
 
-    factor = lax.rsqrt(ar_finish(2, ar_e) / WIDTH + EPS)
-    f_row[...] = factor
-    for b in range(3):
-        fcol[pl.ds(b * 128, 128), :] = spread_rows(factor[b : b + 1, :])
-    for r, (first, count) in enumerate(((0, 64), (64, 64), (128, 128), (256, 128))):
-        part = h_e[pl.ds(first, count), :] * lanes4(fcol[pl.ds(first, count), :])
-        vec[r : r + 1, :] = jnp.sum(part, axis=0, keepdims=True) * gain / count
     for i in (4, 5, 6):
         ig_copy(i, (lo - i + 3 + 4) % 4, x, core).wait_recv()
     for r in range(2):
@@ -403,6 +396,13 @@
             for b in range(4):
                 vec[at : at + 1, b * 128 : b * 128 + 128] = piece[b : b + 1, :]
 
+    factor = lax.rsqrt(ar_finish(2, ar_e) / WIDTH + EPS)
+    f_row[...] = factor
+    for b in range(3):
+        fcol[pl.ds(b * 128, 128), :] = spread_rows(factor[b : b + 1, :])
+    for r, (first, count) in enumerate(((0, 64), (64, 64), (128, 128), (256, 128))):
+        part = h_e[pl.ds(first, count), :] * lanes4(fcol[pl.ds(first, count), :])
+        vec[r : r + 1, :] = jnp.sum(part, axis=0, keepdims=True) * gain / count
     nt = (((1,), (1,)), ((), ()))
     vec_g[...] = vec[0:32, :] * gain
     sims = lax.dot_general(vec_g[...], h_e[...], nt, precision=HI, preferred_element_type=F32)
@@ -686,7 +686,7 @@
         p_resid.reshape(256, COLS),
         w_out,
         w_snap,
-        norm_gain.reshape(1, COLS),
+        norm_gain,
         pass_attn.reshape(STOK, COLS),
         pass_resid.reshape(STOK, COLS),
         pass_len,

time: 135 us -> 134 us (level)
    unnamed x6 -> x4, local copies, waits for them, and re-layouts: 2.93 us -> 2.25 us
where the time goes in v5:
time: 134 us; the launch traced here: 132 us
  Pallas kernels  127 us (95%)
  between operations  2.47 us (2%)
  local copies, waits for them, and re-layouts  2.25 us (2%)
    pallas_call x1, Pallas kernels, shards(): pl.pallas_call(kernel, out_shape=(jax.ShapeDtypeStruct((1, 1), F32), jax....  127 us

profile of v5, /device:TPU:2, one launch (start us, length us, event | category | flops | bytes accessed | tf_op | source)
XLA Modules:
  0.0 131.8 jit_solution(14445003745127997130)
XLA Ops:
  0.6 127.1 %shard_map.139 = (f32[1,1]{1,0:T(1,128)}, f32[128,512]{1,0:T(8,128)}, bf16[2,512]{1,0:T(2,128)(2,1)}) custom-call(bf16[128,512]{1,0:T(8,128)(2,1)} %bitcast.11, bf16[128,512]{1,0:T(8,128)(2,1)} %bitcast.12, bf16[256,512]{1,0:T(8,128)(2,1)} %bitcast.9, bf16[256,512]{1,0:T(8,128)(2,1)} %bitcast.10, bf16[128,512]{1,0:T(8,128)(2,1)} %w_out.1, ...), custom_call_target="tpu_custom_call" | custom-call | tf_op jit(solution)/shard_map/pallas_call | solution.py:623
  128.5 0.0 copy-start
  128.5 1.7 %copy.19 = f32[128,512]{1,0:T(8,128)} copy(f32[128,512]{1,0:T(8,128)} %get-tuple-element.13) | data formatting | bytes 524288
  130.1 0.0 copy-done
  130.1 0.6 copy.20
Async XLA Ops:
  128.5 1.7 %copy-start = (bf16[2,512]{1,0:T(2,128)(2,1)S(1)}, bf16[2,512]{1,0:T(2,128)(2,1)}, u32[]{:S(2)}) copy-start(bf16[2,512]{1,0:T(2,128)(2,1)} %get-tuple-element.14) | copy-start | bytes 6148
